TPU v7x, 32 devices: a whole 2x2x4 slice. The times are simulated.
32 devices in a mesh: section: 2 (over core), dp: 16 (over z, y, x).
Axes of the slice: x: 2, y: 2, z: 4, core: 2. Of those that a mesh axis runs over, the one named last changes fastest.
Arguments:
- inputs: bfloat16 [2, 16, 512, 768], P(None, 'dp'), may hold values from -6 to 6
- segments: int32 [2, 16, 512], P(None, 'dp'), may hold values from 0 to 3, never falling along the last dimension, each value on 1 to 256 neighbouring positions
- expert_ids: int32 [2, 2, 16, 512, 1], P('section', None, 'dp'), may hold values from 0 to 15; in each aligned block of 512 rows (0 to 511, 512 to 1023, ..., all dimensions but the last counted through in order) at most 48 rows name the same one
- w_query: bfloat16 [2, 768, 768], P('section', 'dp'), may hold values from -0.02734375 to 0.02734375
- w_key: bfloat16 [2, 768, 768], P('section', 'dp'), may hold values from -0.21875 to 0.21875
- w_value: bfloat16 [2, 768, 768], P('section', 'dp'), may hold values from -0.21875 to 0.21875
- w_out_proj: bfloat16 [2, 768, 768], P('section', 'dp'), may hold values from -2.5 to 2.5
- w_router: bfloat16 [2, 768, 16], P('section', 'dp'), may hold values from -0.15625 to 0.15625
- attn_gain: bfloat16 [2, 768], P('section', 'dp'), may hold values from 0.5 to 1.5
- ffn_gain: bfloat16 [2, 768], P('section', 'dp'), may hold values from 0.5 to 1.5
- rel_table: float32 [2, 32, 12], P('section'), may hold values from -4 to 4
- w_expert_in: bfloat16 [2, 768, 49152], P('section', None, 'dp'), may hold values from -0.21875 to 0.21875
- w_expert_out: bfloat16 [2, 49152, 768], P('section', 'dp'), may hold values from -2.5 to 2.5
- grad_out: bfloat16 [2, 16, 512, 768], P(None, 'dp'), may hold values from -6 to 6
Outputs:
- layer_out: bfloat16 [2, 2, 16, 512, 768], P('section', None, 'dp')
- grad_in: bfloat16 [2, 2, 16, 512, 768], P('section', None, 'dp')
- grad_query: float32 [2, 768, 768], P('section', 'dp')
- grad_key: float32 [2, 768, 768], P('section', 'dp')
- grad_value: float32 [2, 768, 768], P('section', 'dp')
- grad_out_proj: float32 [2, 768, 768], P('section', 'dp')
- grad_router: float32 [2, 768, 16], P('section', 'dp')
- grad_attn_gain: float32 [2, 768], P('section', 'dp')
- grad_ffn_gain: float32 [2, 768], P('section', 'dp')
- grad_table: float32 [2, 32, 12], P('section')
- grad_expert_in: float32 [2, 768, 49152], P('section', None, 'dp')
- grad_expert_out: float32 [2, 49152, 768], P('section', 'dp')
Inputs may be any that keep to these rules, and one draw needn't show every extreme that they name: `expert_ids`: in each aligned block of 512 rows (one index of dp, one micro-batch, one layer), no expert is named more than 48 times. `segments`: ids never fall along a sequence; a document has 1 to 256 tokens.
All inputs are finite; a program needn't handle non-finite values.
Results may differ from a plain program's by a relative error of at most 0.022.
Values may be sent and summed in bfloat16 or wider, within the bound.
A program may use at most 448 MiB of HBM per device.

v0:
```python
import jax
import jax.numpy as jnp
from jax import lax
from jax.sharding import PartitionSpec as P

EXPERTS = 16
BUCKETS = 32
CAP = 48


norm_eps = 1e-06
distance_marks = (1, 2, 3, 4, 5, 6, 7, 8, 12, 16, 23, 32, 46, 64, 91)
masked_score = -1e30
query_rows = 512
highest = lax.Precision.HIGHEST


def shifted(value, axis, steps):
    count = lax.axis_size(axis)
    pairs = [(source, (source + steps) % count) for source in range(count)]
    return lax.ppermute(value, axis, pairs)


def normed(hidden, gain):
    return hidden * lax.rsqrt(jnp.mean(hidden * hidden, axis=-1, keepdims=True) + norm_eps) * gain


def bucket_of(offset):
    distance = jnp.abs(offset)
    bucket = jnp.zeros(offset.shape, jnp.int32)
    for marker in distance_marks:
        bucket = bucket + (distance >= marker).astype(jnp.int32)
    return bucket + BUCKETS // 2 * (offset > 0).astype(jnp.int32)


def offset_table(length):
    offsets = jnp.arange(2 * length - 1, dtype=jnp.int32) - (length - 1)
    return (bucket_of(offsets)[:, None] == jnp.arange(BUCKETS, dtype=jnp.int32)[None, :]).astype(
        jnp.float32
    )


def bias_blocks(table, length, row_block):
    by_offset = jnp.dot(offset_table(length), table, precision=highest)
    head_count = table.shape[1]
    padded_len = 2 * length + 1
    padded = jnp.pad(by_offset.T, ((0, 0), (0, 2)))
    repeated = jnp.broadcast_to(padded[:, None, :], (head_count, row_block, padded_len))
    repeated = repeated.reshape(head_count, row_block * padded_len)[
        :, : row_block * (padded_len - 1)
    ]
    skewed = repeated.reshape(head_count, row_block, padded_len - 1)
    return [skewed[:, :, length - 1 : 2 * length - 1]]


def offset_terms(score_grad, length, row_start):
    head_count, row_block, _ = score_grad.shape
    padded_len = 2 * length + 1
    placed = jnp.pad(score_grad, ((0, 0), (0, 0), (length - 1 - row_start, row_start + 1)))
    flattened = jnp.pad(
        placed.reshape(head_count, row_block * (padded_len - 1)), ((0, 0), (0, row_block))
    )
    return jnp.sum(flattened.reshape(head_count, row_block, padded_len), axis=1)


def block_scores(query, key_rows, segment, bias, row_start, row_block):
    scores = (
        jnp.einsum("sqhd,skhd->shqk", query, key_rows, preferred_element_type=jnp.float32)
        + bias[None]
    )
    same_doc = segment[:, row_start : row_start + row_block, None] == segment[:, None, :]
    return jnp.where(same_doc[:, None], scores, masked_score)


def attend_forward(query, key_rows, value_rows, segment, biases, row_block):
    contexts = []
    totals = []
    for number, row_start in enumerate(range(0, query.shape[1], row_block)):
        scores = block_scores(query, key_rows, segment, biases[number], row_start, row_block)
        row_max = jnp.max(scores, axis=-1, keepdims=True)
        log_total = row_max + jnp.log(jnp.sum(jnp.exp(scores - row_max), axis=-1, keepdims=True))
        attn_prob = jnp.exp(scores - log_total).astype(jnp.bfloat16)
        contexts.append(
            jnp.einsum(
                "shqk,skhd->sqhd", attn_prob, value_rows, preferred_element_type=jnp.float32
            ).astype(jnp.bfloat16)
        )
        totals.append(log_total)
    return (contexts[0], totals)


def attend_backward(
    query, key_rows, value_rows, segment, biases, totals, context_grad, row_block, offset_sum
):
    length = query.shape[1]
    query_parts = []
    key_grad = jnp.zeros(key_rows.shape, jnp.float32)
    value_grad = jnp.zeros(value_rows.shape, jnp.float32)
    for number, row_start in enumerate(range(0, length, row_block)):
        scores = block_scores(query, key_rows, segment, biases[number], row_start, row_block)
        attn_prob = jnp.exp(scores - totals[number])
        value_grad = jnp.einsum(
            "shqk,sqhd->skhd",
            attn_prob.astype(jnp.bfloat16),
            context_grad,
            preferred_element_type=jnp.float32,
        )
        prob_grad = jnp.einsum(
            "sqhd,skhd->shqk", context_grad, value_rows, preferred_element_type=jnp.float32
        )
        score_grad = (
            attn_prob * (prob_grad - jnp.sum(prob_grad * attn_prob, axis=-1, keepdims=True))
        ).astype(jnp.bfloat16)
        offset_sum = offset_sum + offset_terms(
            jnp.sum(score_grad.astype(jnp.float32), axis=0), length, row_start
        )
        query_parts.append(
            jnp.einsum("shqk,skhd->sqhd", score_grad, key_rows, preferred_element_type=jnp.float32)
        )
        key_grad = jnp.einsum(
            "shqk,sqhd->skhd", score_grad, query, preferred_element_type=jnp.float32
        )
    return (query_parts[0], key_grad, value_grad, offset_sum)


def slot_ids(expert_of):
    chosen = (expert_of[:, None] == jnp.arange(EXPERTS, dtype=jnp.int32)[None, :]).astype(jnp.int32)
    order_in = jnp.sum((jnp.cumsum(chosen, axis=0) - 1) * chosen, axis=1)
    return expert_of * CAP + order_in


def pass_section(values):
    return shifted(values, "section", 1)


def local(
    inputs,
    segments,
    expert_ids,
    w_query,
    w_key,
    w_value,
    w_out_proj,
    w_router,
    attn_gain,
    ffn_gain,
    rel_table,
    w_expert_in,
    w_expert_out,
    grad_out,
):
    section_index = lax.axis_index("section")
    groups = lax.axis_size("dp") // EXPERTS
    micro_count, seq_count, length, model_width = inputs.shape
    head_count = rel_table.shape[2]
    head_size = model_width // head_count
    row_block = min(query_rows, length)
    token_rows = seq_count * length
    shape_heads = (seq_count, length, head_count, head_size)
    expert_in = w_expert_in[0]
    expert_out = w_expert_out[0]
    routing = expert_ids[0, :, :, :, 0]
    shard_tuple = (
        w_query[0],
        w_key[0],
        w_value[0],
        w_out_proj[0],
        w_router[0],
        attn_gain[0],
        ffn_gain[0],
    )
    dense_set = (
        lax.all_gather(shard_tuple[0], "dp", axis=0, tiled=True),
        lax.all_gather(shard_tuple[1], "dp", axis=0, tiled=True),
        lax.all_gather(shard_tuple[2], "dp", axis=0, tiled=True),
        lax.all_gather(shard_tuple[3], "dp", axis=0, tiled=True),
        lax.all_gather(shard_tuple[4], "dp", axis=0, tiled=True),
        lax.all_gather(shard_tuple[5], "dp", axis=0, tiled=True),
        lax.all_gather(shard_tuple[6], "dp", axis=0, tiled=True),
    )
    biases = bias_blocks(rel_table[0], length, row_block)
    owner_in, owner_out = (expert_in, expert_out)

    def to_owners(buffer):
        return jnp.broadcast_to(
            buffer.reshape(EXPERTS, 1, CAP, model_width), (EXPERTS, groups, CAP, model_width)
        ).reshape(EXPERTS * groups, CAP, model_width)

    def from_owners(returned):
        return (
            jnp.sum(returned.reshape(EXPERTS, groups, CAP, model_width), axis=1)
            .reshape(EXPERTS * CAP, model_width)
            .astype(jnp.bfloat16)
        )

    def pick_micro(stacked, moment):
        which = jnp.clip(moment - section_index, 0, micro_count - 1)
        return lax.dynamic_index_in_dim(stacked, which, 0, keepdims=False)

    arriving = jnp.zeros((seq_count, length, model_width), jnp.bfloat16)
    forward_outs = []
    retained_all = []
    for moment in range(micro_count + 1):
        if moment < micro_count:
            first_in = inputs[moment]
        else:
            first_in = jnp.zeros_like(arriving)
        layer_in = (
            jnp.where(section_index == 0, first_in, arriving)
            .astype(jnp.float32)
            .reshape(token_rows, model_width)
        )
        segment = pick_micro(segments, moment)
        expert_of = pick_micro(routing, moment).reshape(token_rows)
        (
            forward_query_weight,
            forward_key_weight,
            forward_value_weight,
            forward_out_weight,
            forward_router_weight,
            forward_gain_attn,
            forward_gain_ffn,
        ) = dense_set
        forward_attn_in = normed(layer_in, forward_gain_attn.astype(jnp.float32)).astype(
            jnp.bfloat16
        )
        forward_query = jnp.dot(
            forward_attn_in, forward_query_weight, preferred_element_type=jnp.float32
        ).astype(jnp.bfloat16)
        forward_key_proj = jnp.dot(
            forward_attn_in, forward_key_weight, preferred_element_type=jnp.float32
        ).astype(jnp.bfloat16)
        forward_value_proj = jnp.dot(
            forward_attn_in, forward_value_weight, preferred_element_type=jnp.float32
        ).astype(jnp.bfloat16)
        forward_context, forward_totals = attend_forward(
            forward_query.reshape(shape_heads),
            forward_key_proj.reshape(shape_heads),
            forward_value_proj.reshape(shape_heads),
            segment,
            biases,
            row_block,
        )
        forward_context = forward_context.reshape(token_rows, model_width)
        forward_after_attn = layer_in + jnp.dot(
            forward_context, forward_out_weight, preferred_element_type=jnp.float32
        )
        forward_ffn_in = normed(forward_after_attn, forward_gain_ffn.astype(jnp.float32)).astype(
            jnp.bfloat16
        )
        forward_router_prob = jax.nn.softmax(
            jnp.dot(forward_ffn_in, forward_router_weight, preferred_element_type=jnp.float32),
            axis=-1,
        )
        forward_chosen = (
            expert_of[:, None] == jnp.arange(EXPERTS, dtype=jnp.int32)[None, :]
        ).astype(jnp.float32)
        forward_gating = jnp.sum(forward_router_prob * forward_chosen, axis=-1)
        forward_slots = slot_ids(expert_of)
        forward_buffer = (
            jnp.zeros((EXPERTS * CAP, model_width), jnp.bfloat16)
            .at[forward_slots]
            .set(forward_ffn_in)
        )
        owner_arrived = lax.all_to_all(
            to_owners(forward_buffer), "dp", split_axis=0, concat_axis=0, tiled=True
        )
        owner_hidden = jnp.einsum(
            "ncd,df->ncf", owner_arrived, owner_in, preferred_element_type=jnp.float32
        )
        owner_active = jax.nn.gelu(owner_hidden).astype(jnp.bfloat16)
        produced = jnp.einsum(
            "ncf,fd->ncd", owner_active, owner_out, preferred_element_type=jnp.float32
        )
        owner_returned = lax.all_to_all(
            produced.astype(jnp.bfloat16), "dp", split_axis=0, concat_axis=0, tiled=True
        ).astype(produced.dtype)
        forward_expert_rows = jnp.take(from_owners(owner_returned), forward_slots, axis=0).astype(
            jnp.float32
        )
        layer_result = forward_after_attn + forward_gating[:, None] * forward_expert_rows
        retained = (
            layer_in,
            forward_attn_in,
            forward_query,
            forward_key_proj,
            forward_value_proj,
            forward_totals,
            forward_context,
            forward_after_attn,
            forward_ffn_in,
            forward_router_prob,
            forward_chosen,
            forward_gating,
            forward_slots,
            forward_expert_rows,
            owner_arrived,
            owner_hidden,
        )
        layer_result, retained = (layer_result, retained)
        out_low = layer_result.astype(jnp.bfloat16).reshape(seq_count, length, model_width)
        forward_outs.append(out_low)
        retained_all.append((segment, retained))
        if moment < micro_count:
            arriving = pass_section(out_low)
    square_zero = jnp.zeros((model_width, model_width), jnp.float32)
    gain_zero = jnp.zeros((model_width,), jnp.float32)
    sums = (
        square_zero,
        square_zero,
        square_zero,
        square_zero,
        jnp.zeros((model_width, EXPERTS), jnp.float32),
        gain_zero,
        gain_zero,
        jnp.zeros((head_count, 2 * length + 1), jnp.float32),
        jnp.zeros(owner_in.shape, jnp.float32),
        jnp.zeros(owner_out.shape, jnp.float32),
    )
    returning = jnp.zeros((seq_count, length, model_width), jnp.bfloat16)
    input_grads = []
    for turn in range(micro_count + 1):
        moment = micro_count - turn
        if moment > 0:
            cotangent = grad_out[moment - 1]
        else:
            cotangent = jnp.zeros_like(returning)
        out_grad = (
            jnp.where(section_index == 1, cotangent, returning)
            .astype(jnp.float32)
            .reshape(token_rows, model_width)
        )
        segment, retained = retained_all[moment]
        (
            backward_layer_in,
            attn_in,
            query,
            key_proj,
            value_proj,
            totals,
            context,
            after_attn,
            ffn_in,
            router_prob,
            chosen,
            gating,
            slots,
            expert_rows,
            arrived,
            hidden,
        ) = retained
        query_weight, key_weight, value_weight, out_weight, router_weight, gain_attn, gain_ffn = (
            dense_set
        )
        (
            backward_sum_query,
            backward_sum_key,
            backward_sum_value,
            backward_sum_out,
            backward_sum_router,
            backward_sum_gain_attn,
            backward_sum_gain_ffn,
            backward_sum_offset,
            backward_sum_in,
            backward_sum_expert_out,
        ) = sums
        gate_grad = jnp.sum(out_grad * expert_rows, axis=-1)
        expert_grad = (out_grad * gating[:, None]).astype(jnp.bfloat16)
        grad_buffer = (
            jnp.zeros((EXPERTS * CAP, model_width), jnp.bfloat16).at[slots].set(expert_grad)
        )
        arrived_grad = lax.all_to_all(
            to_owners(grad_buffer), "dp", split_axis=0, concat_axis=0, tiled=True
        )
        active, gelu_pull = jax.vjp(jax.nn.gelu, hidden)
        backward_sum_expert_out = backward_sum_expert_out + jnp.einsum(
            "ncf,ncd->fd",
            active.astype(jnp.bfloat16),
            arrived_grad,
            preferred_element_type=jnp.float32,
        )
        active_grad = jnp.einsum(
            "ncd,fd->ncf", arrived_grad, owner_out, preferred_element_type=jnp.float32
        )
        hidden_grad = gelu_pull(active_grad)[0].astype(jnp.bfloat16)
        backward_sum_in = backward_sum_in + jnp.einsum(
            "ncd,ncf->df", arrived, hidden_grad, preferred_element_type=jnp.float32
        )
        produced_grad = jnp.einsum(
            "ncf,df->ncd", hidden_grad, owner_in, preferred_element_type=jnp.float32
        )
        returned_grad = lax.all_to_all(
            produced_grad.astype(jnp.bfloat16), "dp", split_axis=0, concat_axis=0, tiled=True
        ).astype(produced_grad.dtype)
        logit_grad = (router_prob * (chosen - gating[:, None]) * gate_grad[:, None]).astype(
            jnp.bfloat16
        )
        backward_sum_router = backward_sum_router + jnp.einsum(
            "td,te->de", ffn_in, logit_grad, preferred_element_type=jnp.float32
        )
        slot_part = jnp.take(from_owners(returned_grad), slots, axis=0).astype(jnp.float32)
        ffn_in_grad = slot_part + jnp.einsum(
            "te,de->td", logit_grad, router_weight, preferred_element_type=jnp.float32
        )
        norm_pull = jax.vjp(normed, after_attn, gain_ffn.astype(jnp.float32))[1]
        residual_grad, gain_grad = norm_pull(ffn_in_grad)
        backward_sum_gain_ffn = backward_sum_gain_ffn + gain_grad
        after_grad = out_grad + residual_grad
        attn_grad = after_grad.astype(jnp.bfloat16)
        backward_sum_out = backward_sum_out + jnp.einsum(
            "td,te->de", context, attn_grad, preferred_element_type=jnp.float32
        )
        context_grad = jnp.einsum(
            "te,de->td", attn_grad, out_weight, preferred_element_type=jnp.float32
        ).astype(jnp.bfloat16)
        query_grad, key_grad, value_grad, backward_sum_offset = attend_backward(
            query.reshape(shape_heads),
            key_proj.reshape(shape_heads),
            value_proj.reshape(shape_heads),
            segment,
            biases,
            totals,
            context_grad.reshape(shape_heads),
            row_block,
            backward_sum_offset,
        )
        query_low = query_grad.reshape(token_rows, model_width).astype(jnp.bfloat16)
        key_low = key_grad.reshape(token_rows, model_width).astype(jnp.bfloat16)
        value_low = value_grad.reshape(token_rows, model_width).astype(jnp.bfloat16)
        backward_sum_query = backward_sum_query + jnp.einsum(
            "td,te->de", attn_in, query_low, preferred_element_type=jnp.float32
        )
        backward_sum_key = backward_sum_key + jnp.einsum(
            "td,te->de", attn_in, key_low, preferred_element_type=jnp.float32
        )
        backward_sum_value = backward_sum_value + jnp.einsum(
            "td,te->de", attn_in, value_low, preferred_element_type=jnp.float32
        )
        attn_in_grad = jnp.einsum(
            "te,de->td", query_low, query_weight, preferred_element_type=jnp.float32
        )
        attn_in_grad = attn_in_grad + jnp.einsum(
            "te,de->td", key_low, key_weight, preferred_element_type=jnp.float32
        )
        attn_in_grad = attn_in_grad + jnp.einsum(
            "te,de->td", value_low, value_weight, preferred_element_type=jnp.float32
        )
        norm_pull = jax.vjp(normed, backward_layer_in, gain_attn.astype(jnp.float32))[1]
        input_grad, gain_grad = norm_pull(attn_in_grad)
        backward_sum_gain_attn = backward_sum_gain_attn + gain_grad
        new_sums = (
            backward_sum_query,
            backward_sum_key,
            backward_sum_value,
            backward_sum_out,
            backward_sum_router,
            backward_sum_gain_attn,
            backward_sum_gain_ffn,
            backward_sum_offset,
            backward_sum_in,
            backward_sum_expert_out,
        )
        layer_grad = after_grad + input_grad
        sums = new_sums
        grad_low = layer_grad.astype(jnp.bfloat16).reshape(seq_count, length, model_width)
        input_grads.append(grad_low)
        if turn < micro_count:
            returning = pass_section(grad_low)
    layer_stack = jnp.stack(
        [
            jnp.where(section_index == 0, forward_outs[number], forward_outs[number + 1])
            for number in range(micro_count)
        ]
    )
    grad_stack = jnp.stack(
        [
            jnp.where(
                section_index == 0,
                input_grads[micro_count - number],
                input_grads[micro_count - number - 1],
            )
            for number in range(micro_count)
        ]
    )
    (
        sum_query,
        sum_key,
        sum_value,
        sum_out,
        sum_router,
        sum_gain_attn,
        sum_gain_ffn,
        sum_offset,
        sum_in,
        sum_expert_out,
    ) = sums
    owned = (
        lax.psum_scatter(sum_query, "dp", scatter_dimension=0, tiled=True),
        lax.psum_scatter(sum_key, "dp", scatter_dimension=0, tiled=True),
        lax.psum_scatter(sum_value, "dp", scatter_dimension=0, tiled=True),
        lax.psum_scatter(sum_out, "dp", scatter_dimension=0, tiled=True),
        lax.psum_scatter(sum_router, "dp", scatter_dimension=0, tiled=True),
        lax.psum_scatter(sum_gain_attn, "dp", scatter_dimension=0, tiled=True),
        lax.psum_scatter(sum_gain_ffn, "dp", scatter_dimension=0, tiled=True),
    )
    table_grad = jnp.dot(
        offset_table(length).T, sum_offset[:, : 2 * length - 1].T, precision=highest
    )
    table_grad = lax.psum(table_grad, "dp")
    return (
        layer_stack[None],
        grad_stack[None],
        owned[0][None],
        owned[1][None],
        owned[2][None],
        owned[3][None],
        owned[4][None],
        owned[5][None],
        owned[6][None],
        table_grad[None],
        sum_in[None],
        sum_expert_out[None],
    )


def solution(mesh):
    return jax.shard_map(
        local,
        mesh=mesh,
        in_specs=(
            P(None, "dp", None, None),
            P(None, "dp", None),
            P("section", None, "dp", None, None),
            P("section", "dp", None),
            P("section", "dp", None),
            P("section", "dp", None),
            P("section", "dp", None),
            P("section", "dp", None),
            P("section", "dp"),
            P("section", "dp"),
            P("section", None, None),
            P("section", None, "dp"),
            P("section", "dp", None),
            P(None, "dp", None, None),
        ),
        out_specs=(
            P("section", None, "dp", None, None),
            P("section", None, "dp", None, None),
            P("section", "dp", None),
            P("section", "dp", None),
            P("section", "dp", None),
            P("section", "dp", None),
            P("section", "dp", None),
            P("section", "dp"),
            P("section", "dp"),
            P("section", None, None),
            P("section", None, "dp"),
            P("section", "dp", None),
        ),
        check_vma=False,
    )
```

profile of v0, /device:TPU:0, one launch (start us, length us, event | category | flops | bytes accessed | tf_op | source)
XLA Modules:
  0.0 1684.0 jit_solution(14318088990686939121)
XLA Ops:
  13.7 43.7 %all-reduce.12 = (bf16[768]{0:T(1024)(128)(2,1)S(1)}, bf16[768]{0:T(1024)(128)(2,1)S(1)}) all-reduce(bf16[768]{0:T(1024)(128)(2,1)S(1)} %dynamic-update-slice, bf16[768]{0:T(1024)(128)(2,1)S(1)} %dynamic-update-slice.1), channel_id=2, replica_groups=mesh['section'=2,'dp'=16] {'dp'}, use_global_device_ids=true, to_apply=%add.7 | all-reduce | flops 1536 | bytes 6144
  71.2 40.9 %reshape.1070 = f32[12,524800]{1,0:T(8,128)} reshape(f32[12,512,1025]{2,1,0:T(8,128)} %broadcast_in_dim.84) | data formatting | bytes 50380800 | tf_op jit(solution)/shard_map/reshape | solution.py:49
  122.8 35.9 %copy.195 = f32[2,8,512,1024]{3,2,1,0:T(8,128)} copy(f32[2,8,512,1024]{3,1,2,0:T(8,128)S(1)} %bitcast.603) | data formatting | bytes 67108864
  158.7 13.4 slice.65
  172.1 12.8 copy.188
  214.6 28.5 %all-gather.18.cloned.1.call-done = bf16[1,768,768]{2,1,0:T(8,128)(2,1)} async-done(((bf16[1,48,768]{2,1,0:T(8,128)(2,1)}), bf16[1,768,768]{2,1,0:T(8,128)(2,1)}) %all-gather.18.cloned.1.call-update) | async-done | bytes 1179664 | tf_op jit(solution)/shard_map/all_gather | solution.py:176
  248.5 32.8 %all_to_all.60 = bf16[16,48,768]{2,1,0:T(8,128)(2,1)S(1)} all-to-all(bf16[16,48,768]{2,1,0:T(8,128)(2,1)S(1)} %bitcast.650), channel_id=1, replica_groups=mesh['section'=2,'dp'=16] {'dp'}, dimensions={0} | all-to-all | bytes 2359296 | tf_op jit(solution)/shard_map/all_to_all | solution.py:265
  304.5 53.9 %all-gather.6 = bf16[1,768,16]{2,0,1:T(2,128)(2,1)S(1)} all-gather(bf16[1,48,16]{2,0,1:T(2,128)(2,1)S(1)} %copy.142), channel_id=8, replica_groups=mesh['section'=2,'dp'=16] {'dp'}, dimensions={1}, use_global_device_ids=true | all-gather | bytes 26112 | tf_op jit(solution)/shard_map/all_gather | solution.py:177
  394.2 33.6 %all_to_all.61 = bf16[16,48,768]{2,1,0:T(8,128)(2,1)S(1)} all-to-all(bf16[16,48,768]{2,1,0:T(8,128)(2,1)S(1)} %bitcast.651), channel_id=1, replica_groups=mesh['section'=2,'dp'=16] {'dp'}, dimensions={0} | all-to-all | bytes 2359296 | tf_op jit(solution)/shard_map/all_to_all | solution.py:265
  454.0 22.9 %all-to-all-done.3 = bf16[16,48,768]{2,1,0:T(8,128)(2,1)S(1)} async-done(((bf16[16,48,768]{2,1,0:T(8,128)(2,1)}), bf16[16,48,768]{2,1,0:T(8,128)(2,1)S(1)}, u32[]{:S(2)}, u32[]{:S(2)}) %all-to-all-start.3) | async-done | bytes 1179680 | tf_op jit(solution)/shard_map/all_to_all | solution.py:275
  522.7 21.9 %all-to-all-done.4 = bf16[16,48,768]{2,1,0:T(8,128)(2,1)} async-done(((bf16[16,48,768]{2,1,0:T(8,128)(2,1)}), bf16[16,48,768]{2,1,0:T(8,128)(2,1)}, u32[]{:S(2)}, u32[]{:S(2)}) %all-to-all-start.4) | async-done | bytes 1179680 | tf_op jit(solution)/shard_map/all_to_all | solution.py:265
  585.7 12.0 fusion.23
  620.7 23.0 %all-to-all-done.7 = bf16[16,48,768]{2,1,0:T(8,128)(2,1)S(1)} async-done(((bf16[16,48,768]{2,1,0:T(8,128)(2,1)}), bf16[16,48,768]{2,1,0:T(8,128)(2,1)S(1)}, u32[]{:S(2)}, u32[]{:S(2)}) %all-to-all-start.7) | async-done | bytes 1179680 | tf_op jit(solution)/shard_map/all_to_all | solution.py:392
  701.7 26.5 %all-to-all-done.8 = bf16[16,48,768]{2,1,0:T(8,128)(2,1)S(1)} async-done(((bf16[16,48,768]{2,1,0:T(8,128)(2,1)}), bf16[16,48,768]{2,1,0:T(8,128)(2,1)S(1)}, u32[]{:S(2)}, u32[]{:S(2)}) %all-to-all-start.8) | async-done | bytes 1179680 | tf_op jit(solution)/shard_map/all_to_all | solution.py:372
  756.4 12.7 fusion.307
  769.1 13.1 all-to-all-done.9
  851.8 31.2 %copy.196 = bf16[2,8,512,1024]{3,1,2,0:T(8,128)(2,1)} copy(bf16[2,8,512,1024]{3,2,1,0:T(8,128)(2,1)S(1)} %bitcast.605) | data formatting | bytes 33554432
  893.3 18.4 %pad_convert_fusion.2 = f32[12,524800]{1,0:T(8,128)} fusion(bf16[12,524288]{1,0:T(8,128)(2,1)} %bitcast.609), kind=kLoop, calls=%fused_computation.14 | loop fusion | flops 6297600 | bytes 37773312 | tf_op jit(solution)/shard_map/reshape | solution.py:63
  920.4 11.8 fusion.9
  950.2 48.4 %reshape.1113 = f32[12,512,1025]{2,1,0:T(8,128)} reshape(f32[12,524800]{1,0:T(8,128)} %pad_convert_fusion.2) | data formatting | bytes 50380800 | tf_op jit(solution)/shard_map/reshape | solution.py:63
  1070.8 12.7 fusion.306
  1108.9 31.5 %copy.197 = bf16[2,8,512,1024]{3,1,2,0:T(8,128)(2,1)} copy(bf16[2,8,512,1024]{3,2,1,0:T(8,128)(2,1)S(1)} %bitcast.606) | data formatting | bytes 33554432
  1146.8 18.3 %pad_convert_fusion.1 = f32[12,524800]{1,0:T(8,128)} fusion(bf16[12,524288]{1,0:T(8,128)(2,1)} %bitcast.607), kind=kLoop, calls=%fused_computation.13 | loop fusion | flops 6297600 | bytes 37773312 | tf_op jit(solution)/shard_map/reshape | solution.py:63
  1165.1 48.7 %reshape.1115 = f32[12,512,1025]{2,1,0:T(8,128)} reshape(f32[12,524800]{1,0:T(8,128)} %pad_convert_fusion.1) | data formatting | bytes 50380800 | tf_op jit(solution)/shard_map/reshape | solution.py:63
  1241.7 12.7 fusion.25
  1254.5 14.7 fusion.24
  1287.8 31.0 %copy.198 = bf16[2,8,512,1024]{3,1,2,0:T(8,128)(2,1)} copy(bf16[2,8,512,1024]{3,2,1,0:T(8,128)(2,1)S(1)} %bitcast.604) | data formatting | bytes 33554432
  1321.1 18.5 %pad_convert_fusion = f32[12,524800]{1,0:T(8,128)} fusion(bf16[12,524288]{1,0:T(8,128)(2,1)} %bitcast.608), kind=kLoop, calls=%fused_computation.12 | loop fusion | flops 6297600 | bytes 37773312 | tf_op jit(solution)/shard_map/reshape | solution.py:63
  1339.6 65.7 %reshape.1117 = f32[12,512,1025]{2,1,0:T(8,128)} reshape(f32[12,524800]{1,0:T(8,128)} %pad_convert_fusion) | data formatting | bytes 50380800 | tf_op jit(solution)/shard_map/reshape | solution.py:63
  1422.0 77.2 %all-reduce.11 = (f32[768]{0:T(1024)S(1)}, f32[768]{0:T(1024)S(1)}, f32[1,32,12]{1,2,0:T(8,128)S(1)}) all-reduce(f32[768]{0:T(1024)S(1)} %add_add_fusion.14, f32[768]{0:T(1024)S(1)} %add_add_fusion.13, f32[1,32,12]{1,2,0:T(8,128)S(1)} %convolution_bitcast_fusion.1), channel_id=14, replica_groups=mesh['section'=2,'dp'=16] {'dp'}, use_global_device_ids=true, to_apply=%region_56.58.clone | all-reduce | flops 1920 | bytes 15360
  1504.3 40.6 %reduce-scatter.12.cloned.1.call-done = f32[48,768]{1,0:T(8,128)} async-done(((f32[768,768]{1,0:T(8,128)}), f32[48,768]{1,0:T(8,128)}) %reduce-scatter.12.cloned.1.call-update) | async-done | bytes 147472 | tf_op jit(solution)/shard_map/reduce_scatter | solution.py:500
  1544.9 132.3 %reduce-scatter.14.cloned.1.call-done = f32[48,768]{1,0:T(8,128)} async-done(((f32[768,768]{1,0:T(8,128)}), f32[48,768]{1,0:T(8,128)}) %reduce-scatter.14.cloned.1.call-update) | async-done | bytes 147472 | tf_op jit(solution)/shard_map/reduce_scatter | solution.py:501
  (716 shorter events, 624.6 us)
Async XLA Ops:
  7.2 182.5 %all-gather.12.cloned.1.call-start = ((), (), s32[]{:S(2)}) async-start(), calls=%async_computation.21 | async-start | bytes 1253376 | tf_op jit(solution)/shard_map/all_gather | solution.py:175
  7.9 184.2 %all-gather.14.cloned.1.call-start = ((), (), s32[]{:S(2)}) async-start(), calls=%async_computation.22 | async-start | bytes 1253376 | tf_op jit(solution)/shard_map/all_gather | solution.py:173
  8.7 188.2 %all-gather.16.cloned.1.call-start = ((), (), s32[]{:S(2)}) async-start(), calls=%async_computation.23 | async-start | bytes 1253376 | tf_op jit(solution)/shard_map/all_gather | solution.py:174
  9.4 233.7 %all-gather.18.cloned.1.call-start = ((), (), s32[]{:S(2)}) async-start(), calls=%async_computation.24 | async-start | bytes 1253376 | tf_op jit(solution)/shard_map/all_gather | solution.py:176
  58.8 138.1 %copy-start.142 = (f32[512]{0:T(512)}, f32[512]{0:T(512)S(1)}, u32[]{:S(2)}) copy-start(f32[512]{0:T(512)S(1)} %fusion.275) | copy-start | bytes 6148
  185.7 174.8 %copy-start.132 = (s32[1,1,1,512,1]{3,4,2,1,0:T(1,128)}, s32[1,1,1,512,1]{3,4,2,1,0:T(1,128)S(1)}, u32[]{:S(2)}) copy-start(s32[1,1,1,512,1]{3,4,2,1,0:T(1,128)S(1)} %get-tuple-element.93) | copy-start | bytes 6148
  185.7 267.2 %copy-start.134 = (s32[1,1,1,512,1]{3,4,2,1,0:T(1,128)}, s32[1,1,1,512,1]{3,4,2,1,0:T(1,128)S(1)}, u32[]{:S(2)}) copy-start(s32[1,1,1,512,1]{3,4,2,1,0:T(1,128)S(1)} %get-tuple-element.94) | copy-start | bytes 6148
  185.7 462.5 %copy-start.130 = (s32[1,1,1,512,1]{3,4,2,1,0:T(1,128)}, s32[1,1,1,512,1]{3,4,2,1,0:T(1,128)S(1)}, u32[]{:S(2)}) copy-start(s32[1,1,1,512,1]{3,4,2,1,0:T(1,128)S(1)} %get-tuple-element.92) | copy-start | bytes 6148
  300.5 61.0 %all-to-all-start.1 = ((bf16[16,48,768]{2,1,0:T(8,128)(2,1)}), bf16[16,48,768]{2,1,0:T(8,128)(2,1)S(1)}, u32[]{:S(2)}, u32[]{:S(2)}) async-start(bf16[16,48,768]{2,1,0:T(8,128)(2,1)} %fusion.134), calls=%async_computation.1 | async-start | bytes 2359296 | tf_op jit(solution)/shard_map/all_to_all | solution.py:275
  364.9 2.4 collective-permute-start
  447.2 29.8 %all-to-all-start.3 = ((bf16[16,48,768]{2,1,0:T(8,128)(2,1)}), bf16[16,48,768]{2,1,0:T(8,128)(2,1)S(1)}, u32[]{:S(2)}, u32[]{:S(2)}) async-start(bf16[16,48,768]{2,1,0:T(8,128)(2,1)} %fusion.137), calls=%async_computation.3 | async-start | bytes 2359296 | tf_op jit(solution)/shard_map/all_to_all | solution.py:275
  482.2 2.5 collective-permute-start.1
  485.0 202.1 %copy-start.175 = (f32[512]{0:T(512)}, f32[512]{0:T(512)S(1)}, u32[]{:S(2)}) copy-start(f32[512]{0:T(512)S(1)} %fusion.279) | copy-start | bytes 6148
  511.1 33.5 %all-to-all-start.4 = ((bf16[16,48,768]{2,1,0:T(8,128)(2,1)}), bf16[16,48,768]{2,1,0:T(8,128)(2,1)}, u32[]{:S(2)}, u32[]{:S(2)}) async-start(bf16[16,48,768]{2,1,0:T(8,128)(2,1)} %bitcast.649), calls=%async_computation.4 | async-start | bytes 2359296 | tf_op jit(solution)/shard_map/all_to_all | solution.py:265
  518.3 129.8 %copy-start.121 = (f32[512,16]{0,1:T(8,128)}, f32[512,16]{0,1:T(8,128)S(1)}, u32[]{:S(2)}) copy-start(f32[512,16]{0,1:T(8,128)S(1)} %get-tuple-element.117) | copy-start | bytes 98308
  518.4 129.8 %copy-start.155 = (f32[512]{0:T(512)}, f32[512]{0:T(512)S(1)}, u32[]{:S(2)}) copy-start(f32[512]{0:T(512)S(1)} %get-tuple-element.116) | copy-start | bytes 6148
  518.4 129.8 %copy-start.164 = (f32[512]{0:T(512)}, f32[512]{0:T(512)S(1)}, u32[]{:S(2)}) copy-start(f32[512]{0:T(512)S(1)} %fusion.246) | copy-start | bytes 6148
  518.4 129.8 %copy-start.149 = (f32[512]{0:T(512)}, f32[512]{0:T(512)S(1)}, u32[]{:S(2)}) copy-start(f32[512]{0:T(512)S(1)} %select_reduce_fusion) | copy-start | bytes 6148
  544.6 33.7 %all-to-all-start.6 = ((bf16[16,48,768]{2,1,0:T(8,128)(2,1)}), bf16[16,48,768]{2,1,0:T(8,128)(2,1)S(1)}, u32[]{:S(2)}, u32[]{:S(2)}) async-start(bf16[16,48,768]{2,1,0:T(8,128)(2,1)} %bitcast.71), calls=%async_computation.6 | async-start | bytes 2359296 | tf_op jit(solution)/shard_map/all_to_all | solution.py:372
  579.4 32.1 %all-to-all-start.5 = ((bf16[16,48,768]{2,1,0:T(8,128)(2,1)}), bf16[16,48,768]{2,1,0:T(8,128)(2,1)S(1)}, u32[]{:S(2)}, u32[]{:S(2)}) async-start(bf16[16,48,768]{2,1,0:T(8,128)(2,1)} %fusion.140), calls=%async_computation.5 | async-start | bytes 2359296 | tf_op jit(solution)/shard_map/all_to_all | solution.py:275
  611.5 32.3 %all-to-all-start.7 = ((bf16[16,48,768]{2,1,0:T(8,128)(2,1)}), bf16[16,48,768]{2,1,0:T(8,128)(2,1)S(1)}, u32[]{:S(2)}, u32[]{:S(2)}) async-start(bf16[16,48,768]{2,1,0:T(8,128)(2,1)} %fusion.125), calls=%async_computation.7 | async-start | bytes 2359296 | tf_op jit(solution)/shard_map/all_to_all | solution.py:392
  687.6 2.4 collective-permute-start.2
  695.0 33.2 %all-to-all-start.8 = ((bf16[16,48,768]{2,1,0:T(8,128)(2,1)}), bf16[16,48,768]{2,1,0:T(8,128)(2,1)S(1)}, u32[]{:S(2)}, u32[]{:S(2)}) async-start(bf16[16,48,768]{2,1,0:T(8,128)(2,1)} %bitcast.86), calls=%async_computation.8 | async-start | bytes 2359296 | tf_op jit(solution)/shard_map/all_to_all | solution.py:372
  749.3 33.0 %all-to-all-start.9 = ((bf16[16,48,768]{2,1,0:T(8,128)(2,1)}), bf16[16,48,768]{2,1,0:T(8,128)(2,1)S(1)}, u32[]{:S(2)}, u32[]{:S(2)}) async-start(bf16[16,48,768]{2,1,0:T(8,128)(2,1)} %fusion.128), calls=%async_computation.9 | async-start | bytes 2359296 | tf_op jit(solution)/shard_map/all_to_all | solution.py:392
  825.4 57.6 %collective-permute-start.3 = (bf16[1,512,768]{2,1,0:T(8,128)(2,1)S(1)}, bf16[1,512,768]{2,1,0:T(8,128)(2,1)S(1)}, u32[]{:S(2)}, u32[]{:S(2)}) collective-permute-start(bf16[1,512,768]{2,1,0:T(8,128)(2,1)S(1)} %bitcast.656), channel_id=1, source_target_pairs={{0,16},{16,0},{1,17},{17,1},{2,18},{18,2},{3,19},{19,3},{4,20},{20... | collective-permute-start | bytes 2359304 | tf_op jit(solution)/shard_map/ppermute | solution.py:21
  886.8 33.6 %all-to-all-start.10 = ((bf16[16,48,768]{2,1,0:T(8,128)(2,1)}), bf16[16,48,768]{2,1,0:T(8,128)(2,1)S(1)}, u32[]{:S(2)}, u32[]{:S(2)}) async-start(bf16[16,48,768]{2,1,0:T(8,128)(2,1)} %bitcast.101), calls=%async_computation.10 | async-start | bytes 2359296 | tf_op jit(solution)/shard_map/all_to_all | solution.py:372
  941.4 82.5 %all-to-all-start.11 = ((bf16[16,48,768]{2,1,0:T(8,128)(2,1)}), bf16[16,48,768]{2,1,0:T(8,128)(2,1)S(1)}, u32[]{:S(2)}, u32[]{:S(2)}) async-start(bf16[16,48,768]{2,1,0:T(8,128)(2,1)} %fusion.131), calls=%async_computation.11 | async-start | bytes 2359296 | tf_op jit(solution)/shard_map/all_to_all | solution.py:392
  948.5 280.4 %reduce-scatter.16.cloned.1.call-start = ((), (), s32[]{:S(2)}) async-start(), calls=%async_computation.25 | async-start | bytes 417792
  1023.9 480.5 %reduce-scatter.8.cloned.1.call-start = ((), (), s32[]{:S(2)}) async-start(), calls=%async_computation.17 | async-start | bytes 2506752 | tf_op jit(solution)/shard_map/reduce_scatter | solution.py:498
  1060.6 443.8 %reduce-scatter.10.cloned.1.call-start = ((), (), s32[]{:S(2)}) async-start(), calls=%async_computation.18 | async-start | bytes 2506752 | tf_op jit(solution)/shard_map/reduce_scatter | solution.py:499
  1146.8 398.1 %reduce-scatter.12.cloned.1.call-start = ((), (), s32[]{:S(2)}) async-start(), calls=%async_computation.19 | async-start | bytes 2506752 | tf_op jit(solution)/shard_map/reduce_scatter | solution.py:500
  1240.5 436.7 %reduce-scatter.14.cloned.1.call-start = ((), (), s32[]{:S(2)}) async-start(), calls=%async_computation.20 | async-start | bytes 2506752 | tf_op jit(solution)/shard_map/reduce_scatter | solution.py:501
  (218 other events, 2037.6 us)
Sparse Core Ops, SparseCore 0:
  10.8 58.8 all-gather.11
  72.5 54.9 all-gather.13
  130.4 54.9 all-gather.15
  188.1 54.9 all-gather.17
  1024.0 122.8 reduce-scatter.15
  1153.0 126.6 reduce-scatter.7
  1285.2 126.6 reduce-scatter.9
  1418.2 126.6 reduce-scatter.11
  1550.4 126.7 reduce-scatter.13
where the time goes:
time: 1690 us; the launch traced here: 1680 us
  local copies, waits for them, and re-layouts  530 us (31%)
  matrix products  335 us (20%)
  waiting for transfers between devices  332 us (20%)
  blocking collectives  241 us (14%)
  other arithmetic  167 us (10%)
  starting transfers between devices  60.9 us (4%)
  between operations  18.2 us (1%)
    unnamed x472, local copies, waits for them, and re-layouts  238 us
    reshape x3, local copies, waits for them, and re-layouts, offset_terms(): return jnp.sum(flattened.reshape(head_count, row_block, padded_len), axis=1)  163 us
    reduce_scatter x1, waiting for transfers between devices, local(): lax.psum_scatter(sum_out, 'dp', scatter_dimension=0, tiled=True)  132 us
    unnamed x2, blocking collectives  121 us
    all_to_all x2, blocking collectives, local(): lax.all_to_all(to_owners(forward_buffer), 'dp', split_axis=0, concat_axis...  66.3 us
    reshape x3, other arithmetic, offset_terms(): return jnp.sum(flattened.reshape(head_count, row_block, padded_len), axis=1)  55.1 us
    all_gather x1, blocking collectives, local(): lax.all_gather(shard_tuple[4], 'dp', axis=0, tiled=True)  53.9 us
    reshape x1, local copies, waits for them, and re-layouts, bias_blocks(): repeated.reshape(head_count, row_block * padded_len)  40.9 us
  transfers between devices with their start and end apart: 23, of which 13 were waited for; matrix products, arithmetic and copies ran while one was open for 45% of the time, Pallas kernels for 0%

commit v1 on v0

v1 whole, which is shorter than its diff:
```python
import jax
import jax.numpy as jnp
from jax import lax
from jax.experimental import pallas as pl
from jax.experimental.pallas import tpu as pltpu
from jax.sharding import PartitionSpec as P

EXPERTS = 16
BUCKETS = 32
CAP = 48


norm_eps = 1e-06
distance_marks = (1, 2, 3, 4, 5, 6, 7, 8, 12, 16, 23, 32, 46, 64, 91)
masked_score = -1e30
highest = lax.Precision.HIGHEST
kernel_params = pltpu.CompilerParams(vmem_limit_bytes=40 * 1024 * 1024)
LANES = 128
SUBLANES = 8


def normed(hidden, gain):
    return hidden * lax.rsqrt(jnp.mean(hidden * hidden, axis=-1, keepdims=True) + norm_eps) * gain


def bucket_of(offset):
    distance = jnp.abs(offset)
    bucket = jnp.zeros(offset.shape, jnp.int32)
    for marker in distance_marks:
        bucket = bucket + (distance >= marker).astype(jnp.int32)
    return bucket + BUCKETS // 2 * (offset > 0).astype(jnp.int32)


def one_hot_buckets(offsets):
    return (bucket_of(offsets)[..., None] == jnp.arange(BUCKETS, dtype=jnp.int32)).astype(
        jnp.float32
    )


def bias_kernel(line_ref, bias_ref):
    length = bias_ref.shape[1]
    rows = jnp.broadcast_to(line_ref[0], (length, 2 * length))
    bias_ref[0] = pltpu.roll(rows, 0, 1, stride=1, stride_axis=0)[:, :length]


def bias_of(table, length):
    heads = table.shape[1]
    turn = jnp.arange(2 * length, dtype=jnp.int32)
    offsets = jnp.where(turn < length, turn, turn - 2 * length)
    line = jnp.dot(one_hot_buckets(offsets), table, precision=highest).T[:, None, :]
    return pl.pallas_call(
        bias_kernel,
        grid=(heads,),
        in_specs=[pl.BlockSpec((1, 1, 2 * length), lambda h: (h, 0, 0))],
        out_specs=pl.BlockSpec((1, length, length), lambda h: (h, 0, 0)),
        out_shape=jax.ShapeDtypeStruct((heads, length, length), jnp.float32),
        compiler_params=kernel_params,
    )(line)


def contract(left, right, left_dim, right_dim):
    return lax.dot_general(
        left, right, (((left_dim,), (right_dim,)), ((), ())), preferred_element_type=jnp.float32
    )


def head_probs(query, key_rows, bias, same_doc):
    scores = contract(query, key_rows, 1, 1) + bias
    scores = jnp.where(same_doc, scores, masked_score)
    weight = jnp.exp(scores - jnp.max(scores, axis=-1, keepdims=True))
    return weight * (1.0 / jnp.sum(weight, axis=-1, keepdims=True))


def forward_kernel(head_size, q_ref, k_ref, v_ref, col_ref, row_ref, bias_ref, context_ref):
    same_doc = col_ref[...] == row_ref[...]
    lane = lax.broadcasted_iota(jnp.int32, q_ref.shape, 1)
    query, key_rows, value_rows = q_ref[...], k_ref[...], v_ref[...]
    result = jnp.zeros(q_ref.shape, jnp.float32)
    for half in range(LANES // head_size):
        own = lane // head_size == half
        prob = head_probs(
            jnp.where(own, query, jnp.zeros_like(query)), key_rows, bias_ref[half], same_doc
        )
        part = contract(prob.astype(jnp.bfloat16), value_rows, 1, 0)
        result = jnp.where(own, part, result)
    context_ref[...] = result.astype(jnp.bfloat16)


def backward_kernel(
    head_size,
    q_ref,
    k_ref,
    v_ref,
    grad_ref,
    col_ref,
    row_ref,
    bias_ref,
    dq_ref,
    dk_ref,
    dv_ref,
    offset_ref,
):
    length = q_ref.shape[0]
    same_doc = col_ref[...] == row_ref[...]
    lane = lax.broadcasted_iota(jnp.int32, q_ref.shape, 1)
    query, key_rows, value_rows, grad = q_ref[...], k_ref[...], v_ref[...], grad_ref[...]
    zero = jnp.zeros(q_ref.shape, jnp.float32)
    dq, dk, dv = zero, zero, zero
    for half in range(LANES // head_size):
        own = lane // head_size == half
        prob = head_probs(
            jnp.where(own, query, jnp.zeros_like(query)), key_rows, bias_ref[half], same_doc
        )
        dv = jnp.where(own, contract(prob.astype(jnp.bfloat16), grad, 0, 0), dv)
        prob_grad = contract(jnp.where(own, grad, jnp.zeros_like(grad)), value_rows, 1, 1)
        score_grad = prob * (prob_grad - jnp.sum(prob_grad * prob, axis=-1, keepdims=True))
        score_low = score_grad.astype(jnp.bfloat16)
        dq = jnp.where(own, contract(score_low, key_rows, 1, 0), dq)
        dk = jnp.where(own, contract(score_low, query, 0, 0), dk)
        rounded = score_low.astype(jnp.float32)
        columns = [jnp.zeros((SUBLANES, LANES), jnp.float32) for _ in range(2 * length // LANES)]
        pad = jnp.zeros((SUBLANES, LANES), jnp.float32)
        tiles = length // LANES
        for block in range(tiles):
            total = jnp.zeros((SUBLANES, length + LANES), jnp.float32)
            for step in range(LANES // SUBLANES):
                start = block * LANES + step * SUBLANES
                wide = jnp.concatenate([rounded[start : start + SUBLANES], pad], axis=1)
                total = total + pltpu.roll(wide, LANES - step * SUBLANES, 1)
            for tile in range(tiles + 1):
                place = tiles - 1 - block + tile
                columns[place] = columns[place] + total[:, tile * LANES : (tile + 1) * LANES]
        offset_ref[half] = jnp.concatenate(columns, axis=1)
    dq_ref[...] = dq.astype(jnp.bfloat16)
    dk_ref[...] = dk.astype(jnp.bfloat16)
    dv_ref[...] = dv.astype(jnp.bfloat16)


def attend_specs(length, width, heads, arrays):
    pair = heads * LANES // width
    wide = pl.BlockSpec((length, LANES), lambda h: (0, h))
    return wide, [wide] * arrays + [
        pl.BlockSpec((length, 1), lambda h: (0, 0)),
        pl.BlockSpec((1, length), lambda h: (0, 0)),
        pl.BlockSpec((pair, length, length), lambda h: (h, 0, 0)),
    ]


def attend_forward(query, key_rows, value_rows, segment, bias):
    length, width = query.shape
    heads = bias.shape[0]
    head_size = width // heads
    wide, in_specs = attend_specs(length, width, heads, 3)
    return pl.pallas_call(
        lambda *refs: forward_kernel(head_size, *refs),
        grid=(width // LANES,),
        in_specs=in_specs,
        out_specs=wide,
        out_shape=jax.ShapeDtypeStruct((length, width), jnp.bfloat16),
        compiler_params=kernel_params,
        cost_estimate=pl.CostEstimate(
            flops=4 * length * length * width,
            bytes_accessed=4 * heads * length * length,
            transcendentals=heads * length * length,
        ),
    )(query, key_rows, value_rows, segment[:, None], segment[None, :], bias)


def attend_backward(query, key_rows, value_rows, grad, segment, bias):
    length, width = query.shape
    heads = bias.shape[0]
    head_size = width // heads
    wide, in_specs = attend_specs(length, width, heads, 4)
    low = jax.ShapeDtypeStruct((length, width), jnp.bfloat16)
    return pl.pallas_call(
        lambda *refs: backward_kernel(head_size, *refs),
        grid=(width // LANES,),
        in_specs=in_specs,
        out_specs=[
            wide,
            wide,
            wide,
            pl.BlockSpec((LANES // head_size, SUBLANES, 2 * length), lambda h: (h, 0, 0)),
        ],
        out_shape=[
            low,
            low,
            low,
            jax.ShapeDtypeStruct((heads, SUBLANES, 2 * length), jnp.float32),
        ],
        compiler_params=kernel_params,
        cost_estimate=pl.CostEstimate(
            flops=10 * length * length * width,
            bytes_accessed=4 * heads * length * length,
            transcendentals=heads * length * length,
        ),
    )(query, key_rows, value_rows, grad, segment[:, None], segment[None, :], bias)


def table_sums(offset_sum):
    heads, rows, places = offset_sum.shape
    offsets = (
        jnp.arange(places, dtype=jnp.int32)[None, :]
        - places // 2
        - jnp.arange(rows, dtype=jnp.int32)[:, None]
    )
    chosen = one_hot_buckets(offsets).reshape(rows * places, BUCKETS)
    return jnp.dot(offset_sum.reshape(heads, rows * places), chosen, precision=highest).T


def dot32(left, right):
    return jnp.dot(left, right, preferred_element_type=jnp.float32)


def routes(expert_of):
    tokens = expert_of.shape[0]
    chosen = expert_of[:, None] == jnp.arange(EXPERTS, dtype=jnp.int32)[None, :]
    place = jnp.arange(tokens, dtype=jnp.int32)
    earlier = (place[:, None] > place[None, :]).astype(jnp.bfloat16)
    before = dot32(earlier, chosen.astype(jnp.bfloat16))
    order_in = jnp.sum(jnp.where(chosen, before, 0.0), axis=1).astype(jnp.int32)
    slots = expert_of * CAP + order_in
    spread = slots[:, None] == jnp.arange(EXPERTS * CAP, dtype=jnp.int32)[None, :]
    return chosen.astype(jnp.float32), spread.astype(jnp.bfloat16)


def swapped(value):
    return lax.ppermute(value, "section", [(0, 1), (1, 0)])


def local(
    inputs,
    segments,
    expert_ids,
    w_query,
    w_key,
    w_value,
    w_out_proj,
    w_router,
    attn_gain,
    ffn_gain,
    rel_table,
    w_expert_in,
    w_expert_out,
    grad_out,
):
    section = lax.axis_index("section")
    first = section == 0
    dp_size = lax.axis_size("dp")
    groups = dp_size // EXPERTS
    length, width = inputs.shape[2:]
    heads = rel_table.shape[2]
    shard_rows = w_query.shape[1]

    def by_micro(stacked):
        return lax.dynamic_index_in_dim(stacked, section, 0, keepdims=False)

    def of_layers(own, other):
        return jnp.where(first, own, other), jnp.where(first, other, own)

    small = jnp.concatenate(
        [
            w_router[0],
            attn_gain[0][:, None],
            ffn_gain[0][:, None],
            jnp.zeros((shard_rows, LANES - EXPERTS - 2), jnp.bfloat16),
        ],
        axis=1,
    )
    lead = jnp.concatenate([w_query[0], w_key[0], small], axis=1)
    rest = jnp.concatenate([w_value[0], w_out_proj[0], small], axis=1)
    shard_keep = jnp.where(first, lead, rest)
    shard_got = swapped(jnp.where(first, rest, lead))
    dense = []
    for shard in of_layers(shard_keep, shard_got):
        mine = lax.all_gather(shard, "dp", axis=0, tiled=True)
        theirs = swapped(mine)
        head_part, tail_part = of_layers(mine, theirs)
        dense.append(
            (
                head_part[:, :width],
                head_part[:, width : 2 * width],
                tail_part[:, :width],
                tail_part[:, width : 2 * width],
                head_part[:, 2 * width : 2 * width + EXPERTS],
                head_part[:, 2 * width + EXPERTS].astype(jnp.float32),
                head_part[:, 2 * width + EXPERTS + 1].astype(jnp.float32),
            )
        )

    segment = by_micro(segments)[0]
    ids = expert_ids[0, :, 0, :, 0]
    ids_keep = by_micro(ids)
    ids_got = swapped(lax.dynamic_index_in_dim(ids, 1 - section, 0, keepdims=False))
    routing = [routes(expert_of) for expert_of in of_layers(ids_keep, ids_got)]
    biases = [
        bias_of(table, length) for table in of_layers(rel_table[0], swapped(rel_table[0]))
    ]
    experts_in = of_layers(w_expert_in[0], swapped(w_expert_in[0]))
    experts_out = of_layers(w_expert_out[0], swapped(w_expert_out[0]))

    def exchanged(buffer):
        return lax.all_to_all(buffer, "dp", split_axis=0, concat_axis=0, tiled=True)

    def to_owners(rows):
        spread_rows = jnp.broadcast_to(
            rows.reshape(EXPERTS, 1, CAP, width), (EXPERTS, groups, CAP, width)
        )
        return exchanged(spread_rows.reshape(EXPERTS * groups, CAP, width)).reshape(-1, width)

    def from_owners(produced):
        returned = exchanged(
            produced.astype(jnp.bfloat16).reshape(EXPERTS * groups, CAP, width)
        ).astype(jnp.float32)
        return (
            jnp.sum(returned.reshape(EXPERTS, groups, CAP, width), axis=1)
            .reshape(EXPERTS * CAP, width)
            .astype(jnp.bfloat16)
        )

    def to_slots(spread, rows):
        return contract(spread, rows, 0, 0).astype(jnp.bfloat16)

    hidden_rows = by_micro(inputs)[0]
    layer_outs = []
    kept = []
    for layer in range(2):
        wq, wk, wv, wo, wr, gain_attn, gain_ffn = dense[layer]
        chosen, spread = routing[layer]
        layer_in = hidden_rows.astype(jnp.float32)
        attn_in = normed(layer_in, gain_attn).astype(jnp.bfloat16)
        query = dot32(attn_in, wq).astype(jnp.bfloat16)
        key_rows = dot32(attn_in, wk).astype(jnp.bfloat16)
        value_rows = dot32(attn_in, wv).astype(jnp.bfloat16)
        context = attend_forward(query, key_rows, value_rows, segment, biases[layer])
        after_attn = layer_in + dot32(context, wo)
        ffn_in = normed(after_attn, gain_ffn).astype(jnp.bfloat16)
        arrived = to_owners(to_slots(spread, ffn_in))
        router_prob = jax.nn.softmax(dot32(ffn_in, wr), axis=-1)
        gating = jnp.sum(router_prob * chosen, axis=-1)
        hidden = dot32(arrived, experts_in[layer])
        active = jax.nn.gelu(hidden).astype(jnp.bfloat16)
        expert_sum = from_owners(dot32(active, experts_out[layer]))
        expert_rows = dot32(spread, expert_sum)
        hidden_rows = (after_attn + gating[:, None] * expert_rows).astype(jnp.bfloat16)
        layer_outs.append(hidden_rows)
        kept.append(
            (
                layer_in,
                attn_in,
                query,
                key_rows,
                value_rows,
                context,
                after_attn,
                ffn_in,
                router_prob,
                gating,
                expert_rows,
                arrived,
                hidden,
                active,
            )
        )

    cotangent = by_micro(grad_out)[0]
    input_grads = [None, None]
    expert_grads = [None, None]
    dense_grads = [None, None]
    for layer in (1, 0):
        wq, wk, wv, wo, wr, gain_attn, gain_ffn = dense[layer]
        chosen, spread = routing[layer]
        (
            layer_in,
            attn_in,
            query,
            key_rows,
            value_rows,
            context,
            after_attn,
            ffn_in,
            router_prob,
            gating,
            expert_rows,
            arrived,
            hidden,
            active,
        ) = kept[layer]
        result_grad = cotangent.astype(jnp.float32)
        expert_grad = (result_grad * gating[:, None]).astype(jnp.bfloat16)
        arrived_grad = to_owners(to_slots(spread, expert_grad))
        gate_grad = jnp.sum(result_grad * expert_rows, axis=-1)
        logit_grad = (router_prob * (chosen - gating[:, None]) * gate_grad[:, None]).astype(
            jnp.bfloat16
        )
        active_grad = contract(arrived_grad, experts_out[layer], 1, 1)
        gelu_pull = jax.vjp(jax.nn.gelu, hidden)[1]
        hidden_grad = gelu_pull(active_grad)[0].astype(jnp.bfloat16)
        slot_grad = from_owners(contract(hidden_grad, experts_in[layer], 1, 1))
        grad_expert_out = contract(active, arrived_grad, 0, 0).astype(jnp.bfloat16)
        grad_expert_in = contract(arrived, hidden_grad, 0, 0).astype(jnp.bfloat16)
        route = [(1 - layer, layer)]
        expert_grads[layer] = (
            (grad_expert_in, lax.ppermute(grad_expert_in, "section", route)),
            (grad_expert_out, lax.ppermute(grad_expert_out, "section", route)),
        )
        ffn_in_grad = dot32(spread, slot_grad) + contract(logit_grad, wr, 1, 1)
        norm_pull = jax.vjp(normed, after_attn, gain_ffn)[1]
        residual_grad, sum_gain_ffn = norm_pull(ffn_in_grad)
        after_grad = result_grad + residual_grad
        attn_grad = after_grad.astype(jnp.bfloat16)
        context_grad = contract(attn_grad, wo, 1, 1).astype(jnp.bfloat16)
        query_grad, key_grad, value_grad, offset_sum = attend_backward(
            query, key_rows, value_rows, context_grad, segment, biases[layer]
        )
        attn_in_grad = (
            contract(query_grad, wq, 1, 1)
            + contract(key_grad, wk, 1, 1)
            + contract(value_grad, wv, 1, 1)
        )
        norm_pull = jax.vjp(normed, layer_in, gain_attn)[1]
        input_grad, sum_gain_attn = norm_pull(attn_in_grad)
        cotangent = (after_grad + input_grad).astype(jnp.bfloat16)
        input_grads[layer] = cotangent
        table_grad = table_sums(offset_sum)
        table_columns = -(-table_grad.size // shard_rows)
        table_block = jnp.pad(
            table_grad.reshape(-1), (0, table_columns * shard_rows - table_grad.size)
        ).reshape(shard_rows, table_columns)
        extra = jnp.concatenate(
            [
                contract(ffn_in, logit_grad, 0, 0),
                sum_gain_attn[:, None],
                sum_gain_ffn[:, None],
                jnp.tile(table_block, (dp_size, 1)),
            ],
            axis=1,
        )
        extra = jnp.pad(extra, ((0, 0), (0, -extra.shape[1] % LANES)))
        lead = jnp.concatenate(
            [contract(attn_in, query_grad, 0, 0), contract(attn_in, key_grad, 0, 0), extra], axis=1
        ).astype(jnp.bfloat16)
        rest = jnp.concatenate(
            [
                contract(attn_in, value_grad, 0, 0),
                contract(context, attn_grad, 0, 0),
                jnp.zeros_like(extra),
            ],
            axis=1,
        ).astype(jnp.bfloat16)
        got = swapped(jnp.where(first, rest, lead))
        both = jnp.where(first, lead, rest).astype(jnp.float32) + got.astype(jnp.float32)
        dense_grads[layer] = lax.psum_scatter(
            both.astype(jnp.bfloat16), "dp", scatter_dimension=0, tiled=True
        )

    def own_layer(pair):
        return jnp.where(first, pair[0], pair[1])

    def other_layer(pair):
        return jnp.where(first, pair[1], pair[0])

    def both_micros(pair):
        mine = own_layer(pair)
        theirs = swapped(other_layer(pair))
        return jnp.stack(of_layers(mine, theirs))[None, :, None]

    def expert_total(which):
        (part0, got0), (part1, got1) = expert_grads[0][which], expert_grads[1][which]
        total = own_layer((part0, part1)).astype(jnp.float32) + own_layer((got0, got1)).astype(
            jnp.float32
        )
        return total[None]

    mine = own_layer(dense_grads)
    theirs = swapped(other_layer(dense_grads))
    lead, rest = (part.astype(jnp.float32) for part in of_layers(mine, theirs))
    extra = lead[:, 2 * width :]
    table_count = BUCKETS * heads
    table_columns = -(-table_count // shard_rows)
    table = extra[:, EXPERTS + 2 : EXPERTS + 2 + table_columns].reshape(-1)[:table_count]
    return (
        both_micros(layer_outs),
        both_micros(input_grads),
        lead[None, :, :width],
        lead[None, :, width : 2 * width],
        rest[None, :, :width],
        rest[None, :, width : 2 * width],
        extra[None, :, :EXPERTS],
        extra[None, :, EXPERTS],
        extra[None, :, EXPERTS + 1],
        table.reshape(1, BUCKETS, heads),
        expert_total(0),
        expert_total(1),
    )


def solution(mesh):
    return jax.shard_map(
        local,
        mesh=mesh,
        in_specs=(
            P(None, "dp", None, None),
            P(None, "dp", None),
            P("section", None, "dp", None, None),
            P("section", "dp", None),
            P("section", "dp", None),
            P("section", "dp", None),
            P("section", "dp", None),
            P("section", "dp", None),
            P("section", "dp"),
            P("section", "dp"),
            P("section", None, None),
            P("section", None, "dp"),
            P("section", "dp", None),
            P(None, "dp", None, None),
        ),
        out_specs=(
            P("section", None, "dp", None, None),
            P("section", None, "dp", None, None),
            P("section", "dp", None),
            P("section", "dp", None),
            P("section", "dp", None),
            P("section", "dp", None),
            P("section", "dp", None),
            P("section", "dp"),
            P("section", "dp"),
            P("section", None, None),
            P("section", None, "dp"),
            P("section", "dp", None),
        ),
        check_vma=False,
    )
```

time: 1690 us -> 878 us (0.52)
  local copies, waits for them, and re-layouts: 530 us -> 52.6 us
  blocking collectives: 241 us -> 0 us
  matrix products: 335 us -> 187 us
  other arithmetic: 167 us -> 60.7 us
  waiting for transfers between devices: 332 us -> 416 us
  Pallas kernels: 0 us -> 64.5 us
    unnamed x472 -> x202, local copies, waits for them, and re-layouts: 238 us -> 32.8 us
    reshape x4 -> x0, local copies, waits for them, and re-layouts: 204 us -> none  [the longest x3 163 us: offset_terms(): return jnp.sum(flattened.reshape(head_count, row_block, padded_len), axis=1)]
    dot_general x83 -> x56, matrix products: 335 us -> 187 us  [the longest x32 123 us: contract(): lax.dot_general(left, right, (((left_dim,), (right_dim,)), ((), ())), pre...]
    unnamed x2 -> x0, blocking collectives: 121 us -> none
    all_gather x4 -> x2, waiting for transfers between devices: 28.6 us -> 117 us  [local(): mine = lax.all_gather(shard, 'dp', axis=0, tiled=True)]
    all_to_all x2 -> x0, blocking collectives: 66.3 us -> none  [local(): lax.all_to_all(to_owners(forward_buffer), 'dp', split_axis=0, concat_axis...]
    pallas_call x0 -> x6, Pallas kernels: none -> 64.5 us  [the longest x2 37.5 us: attend_backward(): pl.pallas_call(lambda *refs: backward_kernel(head_size, *refs), grid=(wid...]
    reshape x3 -> x0, other arithmetic: 55.1 us -> none  [offset_terms(): return jnp.sum(flattened.reshape(head_count, row_block, padded_len), axis=1)]
  transfers between devices with their start and end apart: 23 -> 28, of which waited for: 13 -> 17; matrix products, arithmetic and copies ran while one was open for 45% -> 20% of each run, Pallas kernels for 0% -> 2%
where the time goes in v1:
time: 878 us; the launch traced here: 869 us
  waiting for transfers between devices  416 us (47%)
  matrix products  187 us (21%)
  starting transfers between devices  72.8 us (8%)
  Pallas kernels  64.5 us (7%)
  other arithmetic  60.7 us (7%)
  local copies, waits for them, and re-layouts  52.6 us (6%)
  between operations  15.9 us (2%)
    reduce_scatter x2, waiting for transfers between devices, local(): lax.psum_scatter(both.astype(jnp.bfloat16), 'dp', scatter_dimension=0, ti...  185 us
    dot_general x32, matrix products, contract(): lax.dot_general(left, right, (((left_dim,), (right_dim,)), ((), ())), pre...  123 us
    all_gather x2, waiting for transfers between devices, local(): mine = lax.all_gather(shard, 'dp', axis=0, tiled=True)  117 us
    all_to_all x8, waiting for transfers between devices, exchanged(): return lax.all_to_all(buffer, 'dp', split_axis=0, concat_axis=0, tiled=True)  97.5 us
    dot_general x20, matrix products, dot32(): return jnp.dot(left, right, preferred_element_type=jnp.float32)  61 us
    all_to_all x8, starting transfers between devices, exchanged(): return lax.all_to_all(buffer, 'dp', split_axis=0, concat_axis=0, tiled=True)  51.7 us
    pallas_call x2, Pallas kernels, attend_backward(): pl.pallas_call(lambda *refs: backward_kernel(head_size, *refs), grid=(wid...  37.5 us
    unnamed x202, local copies, waits for them, and re-layouts  32.8 us
  transfers between devices with their start and end apart: 28, of which 17 were waited for; matrix products, arithmetic and copies ran while one was open for 20% of the time, Pallas kernels for 2%

profile of v1, /device:TPU:0, one launch (start us, length us, event | category | flops | bytes accessed | tf_op | source)
XLA Modules:
  0.0 869.4 jit_solution(12080906205433384470)
XLA Ops:
  14.0 66.1 %all-gather.3.cloned.1.call-done = bf16[768,1664]{1,0:T(8,128)(2,1)} async-done(((bf16[48,1664]{1,0:T(8,128)(2,1)}), bf16[768,1664]{1,0:T(8,128)(2,1)}) %all-gather.3.cloned.1.call-update) | async-done | bytes 2555920 | tf_op jit(solution)/shard_map/all_gather | solution.py:276
  102.3 10.9 %shard_map.230 = bf16[512,768]{1,0:T(8,128)(2,1)S(1)} custom-call(bf16[512,768]{1,0:T(8,128)(2,1)S(1)} %convolution_convert_fusion.19.refs_0_, bf16[512,768]{1,0:T(8,128)(2,1)S(1)} %convolution_convert_fusion.18.refs_1_, bf16[512,768]{1,0:T(8,128)(2,1)S(1)} %convolution_convert_fusion.17.refs_2_, s32[512,1]{1,0:T(8,128)S(1)} %copy.97.refs_3_.refs_4_, ...), custom_call_target="tpu_custom_call" | custom-call | flops 805306368 | bytes 12582912 | tf_op jit(solution)/shard_map/pallas_call | solution.py:154
  121.3 50.9 %all-gather.5.cloned.1.call-done = bf16[768,1664]{1,0:T(8,128)(2,1)} async-done(((bf16[48,1664]{1,0:T(8,128)(2,1)}), bf16[768,1664]{1,0:T(8,128)(2,1)}) %all-gather.5.cloned.1.call-update) | async-done | bytes 2555920 | tf_op jit(solution)/shard_map/all_gather | solution.py:276
  182.8 12.4 %fusion.55 = bf16[768,768]{1,0:T(8,128)(2,1)} fusion(bf16[3072,768]{1,0:T(8,128)(2,1)} %collective-permute-done.5, pred[]{:T(512)S(6)} %eq.50, bf16[1,3072,768]{2,1,0:T(8,128)(2,1)} %param.26, f32[768,3072]{1,0:T(8,128)S(1)} %fusion.19), kind=kOutput, calls=%fused_computation.127 | convolution fusion | flops 3648061440 | bytes 20054016 | tf_op jit(solution)/shard_map/dot_general | solution.py:212
  213.2 13.0 %all-to-all-done.1 = bf16[16,48,768]{2,1,0:T(8,128)(2,1)} async-done(((bf16[16,48,768]{2,1,0:T(8,128)(2,1)}), bf16[16,48,768]{2,1,0:T(8,128)(2,1)}, u32[]{:S(2)}, u32[]{:S(2)}) %all-to-all-start.1) | async-done | bytes 1179680 | tf_op jit(solution)/shard_map/all_to_all | solution.py:303
  233.5 11.1 %shard_map.232 = bf16[512,768]{1,0:T(8,128)(2,1)S(1)} custom-call(bf16[512,768]{1,0:T(8,128)(2,1)S(1)} %convolution_convert_fusion.16.refs_0_, bf16[512,768]{1,0:T(8,128)(2,1)S(1)} %convolution_convert_fusion.15.refs_1_, bf16[512,768]{1,0:T(8,128)(2,1)S(1)} %convolution_convert_fusion.14.refs_2_, s32[512,1]{1,0:T(8,128)S(1)} %copy.97.refs_3_.refs_4_, ...), custom_call_target="tpu_custom_call" | custom-call | flops 805306368 | bytes 12582912 | tf_op jit(solution)/shard_map/pallas_call | solution.py:154
  248.9 7.7 all-to-all-start.2
  261.3 23.3 %all-to-all-done.2 = bf16[16,48,768]{2,1,0:T(8,128)(2,1)} async-done(((bf16[16,48,768]{2,1,0:T(8,128)(2,1)}), bf16[16,48,768]{2,1,0:T(8,128)(2,1)}, u32[]{:S(2)}, u32[]{:S(2)}) %all-to-all-start.2) | async-done | bytes 1179680 | tf_op jit(solution)/shard_map/all_to_all | solution.py:303
  284.6 7.9 all-to-all-start.4
  292.5 6.8 fusion.21
  303.0 10.4 %fusion.54 = bf16[768,768]{1,0:T(8,128)(2,1)} fusion(bf16[3072,768]{1,0:T(8,128)(2,1)} %collective-permute-done.5, pred[]{:T(512)S(6)} %eq.50, bf16[1,3072,768]{2,1,0:T(8,128)(2,1)} %param.26, f32[768,3072]{1,0:T(8,128)S(1)} %fusion.21), kind=kOutput, calls=%fused_computation.126 | convolution fusion | flops 3648061440 | bytes 20054016 | tf_op jit(solution)/shard_map/dot_general | solution.py:212
  326.2 13.0 %fusion.13 = bf16[768,3072]{1,0:T(8,128)(2,1)S(1)} fusion(f32[768,3072]{1,0:T(8,128)} %copy-done.92, bf16[768,768]{1,0:T(8,128)(2,1)} %bitcast.30, bf16[3072,768]{1,0:T(8,128)(2,1)} %collective-permute-done.5, pred[]{:T(512)S(6)} %eq.50, bf16[1,3072,768]{2,1,0:T(8,128)(2,1)} %param.26), kind=kOutput, calls=%fused_computation.17 | convolution fusion | flops 3673423872 | bytes 24772608 | tf_op jit(solution)/shard_map/dot_general | solution.py:62
  341.5 7.6 fusion.56
  352.0 6.7 all-to-all-start.5
  365.2 19.6 %all-to-all-done.5 = bf16[16,48,768]{2,1,0:T(8,128)(2,1)} async-done(((bf16[16,48,768]{2,1,0:T(8,128)(2,1)}), bf16[16,48,768]{2,1,0:T(8,128)(2,1)}, u32[]{:S(2)}, u32[]{:S(2)}) %all-to-all-start.5) | async-done | bytes 1179680 | tf_op jit(solution)/shard_map/all_to_all | solution.py:303
  392.6 18.7 %shard_map.233 = (bf16[512,768]{1,0:T(8,128)(2,1)S(1)}, bf16[512,768]{1,0:T(8,128)(2,1)S(1)}, bf16[512,768]{1,0:T(8,128)(2,1)S(1)}, f32[12,8,1024]{2,1,0:T(8,128)S(1)}) custom-call(bf16[512,768]{1,0:T(8,128)(2,1)S(1)} %convolution_convert_fusion.16.refs_0_, bf16[512,768]{1,0:T(8,128)(2,1)S(1)} %copy-done.3, bf16[512,768]{1,0:T(8,128)(2,1)S(1)} %copy-done.5, ...), custom_call_target="tpu_custom_call" | custom-call | flops 2013265920 | bytes 12582912 | tf_op jit(solution)/shard_map/pallas_call | solution.py:175
  426.5 25.3 %all-to-all-done.6 = bf16[16,48,768]{2,1,0:T(8,128)(2,1)} async-done(((bf16[16,48,768]{2,1,0:T(8,128)(2,1)}), bf16[16,48,768]{2,1,0:T(8,128)(2,1)}, u32[]{:S(2)}, u32[]{:S(2)}) %all-to-all-start.6) | async-done | bytes 1179680 | tf_op jit(solution)/shard_map/all_to_all | solution.py:303
  451.8 12.3 %fusion.6 = bf16[768,3072]{1,0:T(8,128)(2,1)S(1)} fusion(f32[768,3072]{1,0:T(8,128)} %copy-done.91, bf16[768,768]{1,0:T(8,128)(2,1)} %bitcast.34, bf16[3072,768]{1,0:T(8,128)(2,1)} %collective-permute-done.5, pred[]{:T(512)S(6)} %eq.50, bf16[1,3072,768]{2,1,0:T(8,128)(2,1)} %param.26), kind=kOutput, calls=%fused_computation.10 | convolution fusion | flops 3673423872 | bytes 24772608 | tf_op jit(solution)/shard_map/dot_general | solution.py:62
  464.1 8.6 fusion.57
  498.9 7.2 all-to-all-done.7
  514.7 18.8 %shard_map.234 = (bf16[512,768]{1,0:T(8,128)(2,1)S(1)}, bf16[512,768]{1,0:T(8,128)(2,1)S(1)}, bf16[512,768]{1,0:T(8,128)(2,1)S(1)}, f32[12,8,1024]{2,1,0:T(8,128)S(1)}) custom-call(bf16[512,768]{1,0:T(8,128)(2,1)S(1)} %convolution_convert_fusion.19.refs_0_, bf16[512,768]{1,0:T(8,128)(2,1)S(1)} %convolution_convert_fusion.18.refs_1_, ...), custom_call_target="tpu_custom_call" | custom-call | flops 2013265920 | bytes 12582912 | tf_op jit(solution)/shard_map/pallas_call | solution.py:175
  547.5 9.8 %broadcast_select_fusion.5 = (bf16[768,1664]{0,1:T(8,128)(2,1)S(1)}, bf16[768,1664]{0,1:T(8,128)(2,1)S(1)}) fusion(pred[]{:T(512)S(6)} %eq.50, bf16[768,768]{0,1:T(8,128)(2,1)S(1)} %copy-done.34, bf16[768,768]{0,1:T(8,128)(2,1)S(1)} %copy-done.48, bf16[1664]{0:T(1024)(128)(2,1)S(1)} %copy-done.70, bf16[768,128]{0,1:T(8,128)(2,1)S(1)} %fusion.126, ...), kind=kLoop, calls=%fused_computation.47 | loop fusion | flops 31948800 | bytes 14945537 | tf_op jit(solution)/shard_map/jit(_where)/select_n | solution.py:451
  565.8 12.6 %add_convert_fusion.1 = (bf16[768,1664]{0,1:T(8,128)(2,1)S(1)}, bf16[768,1664]{0,1:T(8,128)(2,1)}) fusion(bf16[768,1664]{0,1:T(8,128)(2,1)S(1)} %collective-permute-done.9, pred[]{:T(512)S(6)} %eq.50, bf16[768,768]{0,1:T(8,128)(2,1)S(1)} %copy-done.34, bf16[768,768]{0,1:T(8,128)(2,1)S(1)} %copy-done.48, bf16[1664]{0:T(1024)(128)(2,1)S(1)} %copy-done.70, ...), kind=kLoop, calls=%fused_computation.23 | loop fusion | flops 42172416 | bytes 20057344 | tf_op jit(solution)/shard_map/convert_element_type | solution.py:454
  583.0 8.9 %convolution_convert_fusion.2 = bf16[768,3072]{1,0:T(8,128)(2,1)} fusion(bf16[768,768]{1,0:T(8,128)(2,1)} %bitcast.20, bf16[768,3072]{1,0:T(8,128)(2,1)} %copy-done.93), kind=kOutput, calls=%fused_computation.26 | convolution fusion | flops 3626237952 | bytes 10616832 | tf_op jit(solution)/shard_map/dot_general | solution.py:62
  596.3 8.8 %convolution_convert_fusion.3 = bf16[768,3072]{1,0:T(8,128)(2,1)} fusion(bf16[768,768]{1,0:T(8,128)(2,1)} %bitcast.14, bf16[768,3072]{1,0:T(8,128)(2,1)} %copy-done.94), kind=kOutput, calls=%fused_computation.27 | convolution fusion | flops 3626237952 | bytes 10616832 | tf_op jit(solution)/shard_map/dot_general | solution.py:62
  606.4 8.5 convolution_convert_fusion
  614.9 7.4 collective-permute-start.15
  626.5 9.9 %convolution_convert_fusion.1 = bf16[3072,768]{1,0:T(8,128)(2,1)} fusion(bf16[768,768]{1,0:T(8,128)(2,1)} %bitcast.34, f32[768,3072]{1,0:T(8,128)} %copy-done.91), kind=kOutput, calls=%fused_computation.25 | convolution fusion | flops 3647471616 | bytes 15335424 | tf_op jit(solution)/shard_map/dot_general | solution.py:62
  651.0 11.6 %add_bitcast_fusion.1 = f32[1,768,3072]{2,1,0:T(8,128)} fusion(bf16[768,3072]{1,0:T(8,128)(2,1)} %collective-permute-done.12, bf16[768,3072]{1,0:T(8,128)(2,1)} %collective-permute-done.13, bf16[768,3072]{1,0:T(8,128)(2,1)} %convolution_convert_fusion.3, bf16[768,3072]{1,0:T(8,128)(2,1)} %convolution_convert_fusion.2, pred[]{:T(512)S(6)} %eq.50), kind=kLoop, calls=%fused_computation.19 | loop fusion | flops 11796480 | bytes 28311552 | tf_op jit(solution)/shard_map/broadcast_in_dim | solution.py:473
  662.6 51.2 %reduce-scatter.9.cloned.1.call-done = bf16[48,1664]{1,0:T(8,128)(2,1)} async-done(((bf16[768,1664]{1,0:T(8,128)(2,1)}), bf16[48,1664]{1,0:T(8,128)(2,1)}) %reduce-scatter.9.cloned.1.call-update) | async-done | bytes 159760 | tf_op jit(solution)/shard_map/reduce_scatter | solution.py:453
  713.9 134.0 %reduce-scatter.7.cloned.1.call-done = bf16[48,1664]{1,0:T(8,128)(2,1)} async-done(((bf16[768,1664]{1,0:T(8,128)(2,1)}), bf16[48,1664]{1,0:T(8,128)(2,1)}) %reduce-scatter.7.cloned.1.call-update) | async-done | bytes 159760 | tf_op jit(solution)/shard_map/reduce_scatter | solution.py:453
  849.0 9.7 %add_bitcast_fusion = f32[1,3072,768]{2,1,0:T(8,128)} fusion(bf16[3072,768]{1,0:T(8,128)(2,1)} %collective-permute-done.14, bf16[3072,768]{1,0:T(8,128)(2,1)} %collective-permute-done.15, bf16[3072,768]{1,0:T(8,128)(2,1)} %convolution_convert_fusion.1, bf16[3072,768]{1,0:T(8,128)(2,1)} %convolution_convert_fusion, pred[]{:T(512)S(6)} %eq.50), kind=kLoop, calls=%fused_computation.18 | loop fusion | flops 11796480 | bytes 28311552 | tf_op jit(solution)/shard_map/broadcast_in_dim | solution.py:473
  (370 shorter events, 222.6 us)
Async XLA Ops:
  7.2 72.9 %all-gather.3.cloned.1.call-start = ((), (), s32[]{:S(2)}) async-start(), calls=%async_computation.10 | async-start | bytes 2715648 | tf_op jit(solution)/shard_map/all_gather | solution.py:276
  11.6 1.5 collective-permute-start
  14.0 158.2 %all-gather.5.cloned.1.call-start = ((), (), s32[]{:S(2)}) async-start(), calls=%async_computation.11 | async-start | bytes 2715648 | tf_op jit(solution)/shard_map/all_gather | solution.py:276
  84.7 12.8 %collective-permute-start.1 = (bf16[768,1664]{0,1:T(8,128)(2,1)S(1)}, bf16[768,1664]{0,1:T(8,128)(2,1)}, u32[]{:S(2)}, u32[]{:S(2)}) collective-permute-start(bf16[768,1664]{0,1:T(8,128)(2,1)S(1)} %copy.95), channel_id=1, source_target_pairs={{0,16},{16,0},{1,17},{17,1},{2,18},{18,2},{3,19},{19,3},{4,20},{20... | collective-permute-start | bytes 7667720 | tf_op jit(solution)/shard_map/ppermute | solution.py:228
  84.8 4.4 collective-permute-start.2
  85.3 11.6 %collective-permute-start.3 = (s32[512]{0:T(512)S(1)}, s32[512]{0:T(512)S(1)}, u32[]{:S(2)}, u32[]{:S(2)}) collective-permute-start(s32[512]{0:T(512)S(1)} %bitcast.199), channel_id=1, source_target_pairs={{0,16},{16,0},{1,17},{17,1},{2,18},{18,2},{3,19},{19,3},{4,20},{20... | collective-permute-start | bytes 6152 | tf_op jit(solution)/shard_map/ppermute | solution.py:228
  85.4 97.4 %collective-permute-start.5 = (bf16[3072,768]{1,0:T(8,128)(2,1)}, bf16[3072,768]{1,0:T(8,128)(2,1)}, u32[]{:S(2)}, u32[]{:S(2)}) collective-permute-start(bf16[3072,768]{1,0:T(8,128)(2,1)} %bitcast.204), channel_id=1, source_target_pairs={{0,16},{16,0},{1,17},{17,1},{2,18},{18,2},{3,19},{19,3},{4,20},{20... | collective-permute-start | bytes 14155784 | tf_op jit(solution)/shard_map/ppermute | solution.py:228
  85.8 90.9 %collective-permute-start.4 = (bf16[768,3072]{1,0:T(8,128)(2,1)}, bf16[768,3072]{1,0:T(8,128)(2,1)}, u32[]{:S(2)}, u32[]{:S(2)}) collective-permute-start(bf16[768,3072]{1,0:T(8,128)(2,1)} %bitcast.205), channel_id=1, source_target_pairs={{0,16},{16,0},{1,17},{17,1},{2,18},{18,2},{3,19},{19,3},{4,20},{20... | collective-permute-start | bytes 14155784 | tf_op jit(solution)/shard_map/ppermute | solution.py:228
  96.9 266.0 %copy-start.65 = (s32[512]{0:T(512)}, s32[512]{0:T(512)S(1)}, u32[]{:S(2)}) copy-start(s32[512]{0:T(512)S(1)} %get-tuple-element.118) | copy-start | bytes 6148
  97.4 319.0 %copy-start.77 = (s32[512]{0:T(512)}, s32[512]{0:T(512)S(1)}, u32[]{:S(2)}) copy-start(s32[512]{0:T(512)S(1)} %get-tuple-element.139) | copy-start | bytes 6148
  116.4 60.3 %all-to-all-start = ((bf16[16,48,768]{2,1,0:T(8,128)(2,1)}), bf16[16,48,768]{2,1,0:T(8,128)(2,1)}, u32[]{:S(2)}, u32[]{:S(2)}) async-start(bf16[16,48,768]{2,1,0:T(8,128)(2,1)} %bitcast.185), calls=%async_computation | async-start | bytes 2359296 | tf_op jit(solution)/shard_map/all_to_all | solution.py:303
  176.6 31.4 %collective-permute-start.6 = (bf16[768,1664]{0,1:T(8,128)(2,1)}, bf16[768,1664]{0,1:T(8,128)(2,1)}, u32[]{:S(2)}, u32[]{:S(2)}) collective-permute-start(bf16[768,1664]{0,1:T(8,128)(2,1)} %copy.99), channel_id=1, source_target_pairs={{0,16},{16,0},{1,17},{17,1},{2,18},{18,2},{3,19},{19,3},{4,20},{20... | collective-permute-start | bytes 7667720 | tf_op jit(solution)/shard_map/ppermute | solution.py:228
  195.1 31.0 %all-to-all-start.1 = ((bf16[16,48,768]{2,1,0:T(8,128)(2,1)}), bf16[16,48,768]{2,1,0:T(8,128)(2,1)}, u32[]{:S(2)}, u32[]{:S(2)}) async-start(bf16[16,48,768]{2,1,0:T(8,128)(2,1)} %bitcast.184), calls=%async_computation.1 | async-start | bytes 2359296 | tf_op jit(solution)/shard_map/all_to_all | solution.py:303
  211.6 203.5 %copy-start.68 = (f32[768]{0:T(1024)}, f32[768]{0:T(1024)S(1)}, u32[]{:S(2)}) copy-start(f32[768]{0:T(1024)S(1)} %get-tuple-element.83) | copy-start | bytes 9220
  213.2 203.3 %copy-start.73 = (f32[512]{0:T(512)}, f32[512]{0:T(512)S(1)}, u32[]{:S(2)}) copy-start(f32[512]{0:T(512)S(1)} %select_reduce_fusion.1) | copy-start | bytes 6148
  248.9 35.7 %all-to-all-start.2 = ((bf16[16,48,768]{2,1,0:T(8,128)(2,1)}), bf16[16,48,768]{2,1,0:T(8,128)(2,1)}, u32[]{:S(2)}, u32[]{:S(2)}) async-start(bf16[16,48,768]{2,1,0:T(8,128)(2,1)} %bitcast.188), calls=%async_computation.2 | async-start | bytes 2359296 | tf_op jit(solution)/shard_map/all_to_all | solution.py:303
  284.6 35.1 %all-to-all-start.4 = ((bf16[16,48,768]{2,1,0:T(8,128)(2,1)}), bf16[16,48,768]{2,1,0:T(8,128)(2,1)}, u32[]{:S(2)}, u32[]{:S(2)}) async-start(bf16[16,48,768]{2,1,0:T(8,128)(2,1)} %bitcast.189), calls=%async_computation.4 | async-start | bytes 2359296 | tf_op jit(solution)/shard_map/all_to_all | solution.py:303
  319.6 32.3 %all-to-all-start.3 = ((bf16[16,48,768]{2,1,0:T(8,128)(2,1)}), bf16[16,48,768]{2,1,0:T(8,128)(2,1)}, u32[]{:S(2)}, u32[]{:S(2)}) async-start(bf16[16,48,768]{2,1,0:T(8,128)(2,1)} %bitcast.190), calls=%async_computation.3 | async-start | bytes 2359296 | tf_op jit(solution)/shard_map/all_to_all | solution.py:303
  352.0 32.9 %all-to-all-start.5 = ((bf16[16,48,768]{2,1,0:T(8,128)(2,1)}), bf16[16,48,768]{2,1,0:T(8,128)(2,1)}, u32[]{:S(2)}, u32[]{:S(2)}) async-start(bf16[16,48,768]{2,1,0:T(8,128)(2,1)} %bitcast.186), calls=%async_computation.5 | async-start | bytes 2359296 | tf_op jit(solution)/shard_map/all_to_all | solution.py:303
  419.4 32.4 %all-to-all-start.6 = ((bf16[16,48,768]{2,1,0:T(8,128)(2,1)}), bf16[16,48,768]{2,1,0:T(8,128)(2,1)}, u32[]{:S(2)}, u32[]{:S(2)}) async-start(bf16[16,48,768]{2,1,0:T(8,128)(2,1)} %bitcast.187), calls=%async_computation.6 | async-start | bytes 2359296 | tf_op jit(solution)/shard_map/all_to_all | solution.py:303
  472.7 33.4 %all-to-all-start.7 = ((bf16[16,48,768]{2,1,0:T(8,128)(2,1)}), bf16[16,48,768]{2,1,0:T(8,128)(2,1)}, u32[]{:S(2)}, u32[]{:S(2)}) async-start(bf16[16,48,768]{2,1,0:T(8,128)(2,1)} %bitcast.183), calls=%async_computation.7 | async-start | bytes 2359296 | tf_op jit(solution)/shard_map/all_to_all | solution.py:303
  479.0 234.8 %reduce-scatter.9.cloned.1.call-start = ((), (), s32[]{:S(2)}) async-start(), calls=%async_computation.13 | async-start | bytes 2715648 | tf_op jit(solution)/shard_map/reduce_scatter | solution.py:453
  557.3 4.9 collective-permute-start.9
  557.3 8.5 collective-permute-start.10
  582.9 265.0 %reduce-scatter.7.cloned.1.call-start = ((), (), s32[]{:S(2)}) async-start(), calls=%async_computation.12 | async-start | bytes 2715648 | tf_op jit(solution)/shard_map/reduce_scatter | solution.py:453
  591.9 59.1 %collective-permute-start.13 = (bf16[768,3072]{1,0:T(8,128)(2,1)}, bf16[768,3072]{1,0:T(8,128)(2,1)}, u32[]{:S(2)}, u32[]{:S(2)}) collective-permute-start(bf16[768,3072]{1,0:T(8,128)(2,1)} %convolution_convert_fusion.2), channel_id=1, source_target_pairs={{0,16},{1,17},{2,18},{3,19},{4,20},{5,21},{6,22},{7,23},{8,24},{9,... | collective-permute-start | bytes 14155784 | tf_op jit(solution)/shard_map/ppermute | solution.py:404
  605.1 46.0 %collective-permute-start.12 = (bf16[768,3072]{1,0:T(8,128)(2,1)}, bf16[768,3072]{1,0:T(8,128)(2,1)}, u32[]{:S(2)}, u32[]{:S(2)}) collective-permute-start(bf16[768,3072]{1,0:T(8,128)(2,1)} %convolution_convert_fusion.3), channel_id=1, source_target_pairs={{16,0},{17,1},{18,2},{19,3},{20,4},{21,5},{22,6},{23,7},{24,8},{25... | collective-permute-start | bytes 14155784 | tf_op jit(solution)/shard_map/ppermute | solution.py:404
  614.9 234.0 %collective-permute-start.15 = (bf16[3072,768]{1,0:T(8,128)(2,1)}, bf16[3072,768]{1,0:T(8,128)(2,1)}, u32[]{:S(2)}, u32[]{:S(2)}) collective-permute-start(bf16[3072,768]{1,0:T(8,128)(2,1)} %convolution_convert_fusion), channel_id=1, source_target_pairs={{0,16},{1,17},{2,18},{3,19},{4,20},{5,21},{6,22},{7,23},{8,24},{9,... | collective-permute-start | bytes 14155784 | tf_op jit(solution)/shard_map/ppermute | solution.py:405
  636.3 212.6 %collective-permute-start.14 = (bf16[3072,768]{1,0:T(8,128)(2,1)}, bf16[3072,768]{1,0:T(8,128)(2,1)}, u32[]{:S(2)}, u32[]{:S(2)}) collective-permute-start(bf16[3072,768]{1,0:T(8,128)(2,1)} %convolution_convert_fusion.1), channel_id=1, source_target_pairs={{16,0},{17,1},{18,2},{19,3},{20,4},{21,5},{22,6},{23,7},{24,8},{25... | collective-permute-start | bytes 14155784 | tf_op jit(solution)/shard_map/ppermute | solution.py:405
  637.9 9.3 %collective-permute-start.7 = (bf16[512,768]{1,0:T(8,128)(2,1)S(1)}, bf16[512,768]{1,0:T(8,128)(2,1)S(1)}, u32[]{:S(2)}, u32[]{:S(2)}) collective-permute-start(bf16[512,768]{1,0:T(8,128)(2,1)S(1)} %copy-done.61), channel_id=1, source_target_pairs={{0,16},{16,0},{1,17},{17,1},{2,18},{18,2},{3,19},{19,3},{4,20},{20... | collective-permute-start | bytes 2359304 | tf_op jit(solution)/shard_map/ppermute | solution.py:228
  647.3 2.3 collective-permute-start.8
  848.9 9.8 %collective-permute-start.11 = (bf16[48,1664]{1,0:T(8,128)(2,1)S(1)}, bf16[48,1664]{1,0:T(8,128)(2,1)S(1)}, u32[]{:S(2)}, u32[]{:S(2)}) collective-permute-start(bf16[48,1664]{1,0:T(8,128)(2,1)S(1)} %broadcast_select_fusion.30), channel_id=1, source_target_pairs={{0,16},{16,0},{1,17},{17,1},{2,18},{18,2},{3,19},{19,3},{4,20},{20... | collective-permute-start | bytes 479240 | tf_op jit(solution)/shard_map/ppermute | solution.py:228
  (94 other events, 1417.9 us)
Sparse Core Ops, SparseCore 0:
  14.0 66.0 all-gather.2
  97.6 74.5 all-gather.4
  583.1 130.7 reduce-scatter.8
  720.0 127.8 reduce-scatter.6

commit v2 on v1

--- a/solution.py
+++ b/solution.py
@@ -450,9 +450,8 @@
         ).astype(jnp.bfloat16)
         got = swapped(jnp.where(first, rest, lead))
         both = jnp.where(first, lead, rest).astype(jnp.float32) + got.astype(jnp.float32)
-        dense_grads[layer] = lax.psum_scatter(
-            both.astype(jnp.bfloat16), "dp", scatter_dimension=0, tiled=True
-        )
+        parts = exchanged(both.astype(jnp.bfloat16).reshape(dp_size, shard_rows, -1))
+        dense_grads[layer] = jnp.sum(parts.astype(jnp.float32), axis=0)
 
     def own_layer(pair):
         return jnp.where(first, pair[0], pair[1])

time: 878 us -> 742 us (0.85)
  waiting for transfers between devices: 416 us -> 254 us
  starting transfers between devices: 72.8 us -> 91.7 us
    reduce_scatter x2 -> x0, waiting for transfers between devices: 185 us -> none  [local(): lax.psum_scatter(both.astype(jnp.bfloat16), 'dp', scatter_dimension=0, ti...]
    all_to_all x8 -> x10, waiting for transfers between devices: 97.5 us -> 118 us  [exchanged(): return lax.all_to_all(buffer, 'dp', split_axis=0, concat_axis=0, tiled=True)]
    all_to_all x8 -> x10, starting transfers between devices: 51.7 us -> 71.8 us  [exchanged(): return lax.all_to_all(buffer, 'dp', split_axis=0, concat_axis=0, tiled=True)]
    unnamed x202 -> x196, local copies, waits for them, and re-layouts: 32.8 us -> 24.3 us
  transfers between devices with their start and end apart: 28 -> 28, of which waited for: 17 -> 17; matrix products, arithmetic and copies ran while one was open for 20% -> 24% of each run, Pallas kernels for 2% -> 2%
where the time goes in v2:
time: 742 us; the launch traced here: 728 us
  waiting for transfers between devices  254 us (34%)
  matrix products  186 us (25%)
  starting transfers between devices  91.7 us (12%)
  Pallas kernels  64.6 us (9%)
  other arithmetic  62 us (8%)
  local copies, waits for them, and re-layouts  52.6 us (7%)
  between operations  16.1 us (2%)
    dot_general x32, matrix products, contract(): lax.dot_general(left, right, (((left_dim,), (right_dim,)), ((), ())), pre...  123 us
    all_gather x2, waiting for transfers between devices, local(): mine = lax.all_gather(shard, 'dp', axis=0, tiled=True)  119 us
    all_to_all x10, waiting for transfers between devices, exchanged(): return lax.all_to_all(buffer, 'dp', split_axis=0, concat_axis=0, tiled=True)  118 us
    all_to_all x10, starting transfers between devices, exchanged(): return lax.all_to_all(buffer, 'dp', split_axis=0, concat_axis=0, tiled=True)  71.8 us
    dot_general x20, matrix products, dot32(): return jnp.dot(left, right, preferred_element_type=jnp.float32)  61 us
    pallas_call x2, Pallas kernels, attend_backward(): pl.pallas_call(lambda *refs: backward_kernel(head_size, *refs), grid=(wid...  37.6 us
    unnamed x196, local copies, waits for them, and re-layouts  24.3 us
    pallas_call x2, Pallas kernels, attend_forward(): pl.pallas_call(lambda *refs: forward_kernel(head_size, *refs), grid=(widt...  22 us
  transfers between devices with their start and end apart: 28, of which 17 were waited for; matrix products, arithmetic and copies ran while one was open for 24% of the time, Pallas kernels for 2%

profile of v2, /device:TPU:0, one launch (start us, length us, event | category | flops | bytes accessed | tf_op | source)
XLA Modules:
  0.0 727.6 jit_solution(4446468381777428669)
XLA Ops:
  14.0 66.1 %all-gather.3.cloned.1.call-done = bf16[768,1664]{1,0:T(8,128)(2,1)} async-done(((bf16[48,1664]{1,0:T(8,128)(2,1)}), bf16[768,1664]{1,0:T(8,128)(2,1)}) %all-gather.3.cloned.1.call-update) | async-done | bytes 2555920 | tf_op jit(solution)/shard_map/all_gather | solution.py:276
  102.4 10.9 %shard_map.230 = bf16[512,768]{1,0:T(8,128)(2,1)S(1)} custom-call(bf16[512,768]{1,0:T(8,128)(2,1)S(1)} %convolution_convert_fusion.19.refs_0_, bf16[512,768]{1,0:T(8,128)(2,1)S(1)} %convolution_convert_fusion.18.refs_1_, bf16[512,768]{1,0:T(8,128)(2,1)S(1)} %convolution_convert_fusion.17.refs_2_, s32[512,1]{1,0:T(8,128)S(1)} %copy.97.refs_3_.refs_4_, ...), custom_call_target="tpu_custom_call" | custom-call | flops 805306368 | bytes 12582912 | tf_op jit(solution)/shard_map/pallas_call | solution.py:154
  121.2 53.1 %all-gather.5.cloned.1.call-done = bf16[768,1664]{1,0:T(8,128)(2,1)} async-done(((bf16[48,1664]{1,0:T(8,128)(2,1)}), bf16[768,1664]{1,0:T(8,128)(2,1)}) %all-gather.5.cloned.1.call-update) | async-done | bytes 2555920 | tf_op jit(solution)/shard_map/all_gather | solution.py:276
  184.9 12.4 %fusion.55 = bf16[768,768]{1,0:T(8,128)(2,1)} fusion(bf16[3072,768]{1,0:T(8,128)(2,1)} %collective-permute-done.5, pred[]{:T(512)S(6)} %eq.50, bf16[1,3072,768]{2,1,0:T(8,128)(2,1)} %param.26, f32[768,3072]{1,0:T(8,128)S(1)} %fusion.19), kind=kOutput, calls=%fused_computation.129 | convolution fusion | flops 3648061440 | bytes 20054016 | tf_op jit(solution)/shard_map/dot_general | solution.py:212
  214.8 13.1 %all-to-all-done.1 = bf16[16,48,768]{2,1,0:T(8,128)(2,1)} async-done(((bf16[16,48,768]{2,1,0:T(8,128)(2,1)}), bf16[16,48,768]{2,1,0:T(8,128)(2,1)}, u32[]{:S(2)}, u32[]{:S(2)}) %all-to-all-start.1) | async-done | bytes 1179680 | tf_op jit(solution)/shard_map/all_to_all | solution.py:303
  235.3 11.1 %shard_map.232 = bf16[512,768]{1,0:T(8,128)(2,1)S(1)} custom-call(bf16[512,768]{1,0:T(8,128)(2,1)S(1)} %convolution_convert_fusion.16.refs_0_, bf16[512,768]{1,0:T(8,128)(2,1)S(1)} %convolution_convert_fusion.15.refs_1_, bf16[512,768]{1,0:T(8,128)(2,1)S(1)} %convolution_convert_fusion.14.refs_2_, s32[512,1]{1,0:T(8,128)S(1)} %copy.97.refs_3_.refs_4_, ...), custom_call_target="tpu_custom_call" | custom-call | flops 805306368 | bytes 12582912 | tf_op jit(solution)/shard_map/pallas_call | solution.py:154
  250.6 8.0 %all-to-all-start.2 = ((bf16[16,48,768]{2,1,0:T(8,128)(2,1)}), bf16[16,48,768]{2,1,0:T(8,128)(2,1)}, u32[]{:S(2)}, u32[]{:S(2)}) async-start(bf16[16,48,768]{2,1,0:T(8,128)(2,1)} %bitcast.190), calls=%async_computation.2 | async-start | bytes 2359296 | tf_op jit(solution)/shard_map/all_to_all | solution.py:303
  263.3 23.2 %all-to-all-done.2 = bf16[16,48,768]{2,1,0:T(8,128)(2,1)} async-done(((bf16[16,48,768]{2,1,0:T(8,128)(2,1)}), bf16[16,48,768]{2,1,0:T(8,128)(2,1)}, u32[]{:S(2)}, u32[]{:S(2)}) %all-to-all-start.2) | async-done | bytes 1179680 | tf_op jit(solution)/shard_map/all_to_all | solution.py:303
  286.5 7.7 %all-to-all-start.4 = ((bf16[16,48,768]{2,1,0:T(8,128)(2,1)}), bf16[16,48,768]{2,1,0:T(8,128)(2,1)}, u32[]{:S(2)}, u32[]{:S(2)}) async-start(bf16[16,48,768]{2,1,0:T(8,128)(2,1)} %bitcast.191), calls=%async_computation.4 | async-start | bytes 2359296 | tf_op jit(solution)/shard_map/all_to_all | solution.py:303
  304.8 10.4 %fusion.54 = bf16[768,768]{1,0:T(8,128)(2,1)} fusion(bf16[3072,768]{1,0:T(8,128)(2,1)} %collective-permute-done.5, pred[]{:T(512)S(6)} %eq.50, bf16[1,3072,768]{2,1,0:T(8,128)(2,1)} %param.26, f32[768,3072]{1,0:T(8,128)S(1)} %fusion.21), kind=kOutput, calls=%fused_computation.128 | convolution fusion | flops 3648061440 | bytes 20054016 | tf_op jit(solution)/shard_map/dot_general | solution.py:212
  327.7 13.0 %fusion.13 = bf16[768,3072]{1,0:T(8,128)(2,1)S(1)} fusion(f32[768,3072]{1,0:T(8,128)} %copy-done.90, bf16[768,768]{1,0:T(8,128)(2,1)} %bitcast.30, bf16[3072,768]{1,0:T(8,128)(2,1)} %collective-permute-done.5, pred[]{:T(512)S(6)} %eq.50, bf16[1,3072,768]{2,1,0:T(8,128)(2,1)} %param.26), kind=kOutput, calls=%fused_computation.17 | convolution fusion | flops 3673423872 | bytes 24772608 | tf_op jit(solution)/shard_map/dot_general | solution.py:62
  343.0 7.6 %fusion.56 = bf16[768,768]{1,0:T(8,128)(2,1)} fusion(bf16[768,3072]{1,0:T(8,128)(2,1)S(1)} %fusion.13, bf16[768,3072]{1,0:T(8,128)(2,1)} %collective-permute-done.4, pred[]{:T(512)S(6)} %eq.50, bf16[1,768,3072]{2,1,0:T(8,128)(2,1)} %param.25), kind=kOutput, calls=%fused_computation.130 | convolution fusion | flops 3626827776 | bytes 15335425 | tf_op jit(solution)/shard_map/dot_general | solution.py:62
  366.8 19.9 %all-to-all-done.5 = bf16[16,48,768]{2,1,0:T(8,128)(2,1)} async-done(((bf16[16,48,768]{2,1,0:T(8,128)(2,1)}), bf16[16,48,768]{2,1,0:T(8,128)(2,1)}, u32[]{:S(2)}, u32[]{:S(2)}) %all-to-all-start.5) | async-done | bytes 1179680 | tf_op jit(solution)/shard_map/all_to_all | solution.py:303
  394.5 18.7 %shard_map.233 = (bf16[512,768]{1,0:T(8,128)(2,1)S(1)}, bf16[512,768]{1,0:T(8,128)(2,1)S(1)}, bf16[512,768]{1,0:T(8,128)(2,1)S(1)}, f32[12,8,1024]{2,1,0:T(8,128)S(1)}) custom-call(bf16[512,768]{1,0:T(8,128)(2,1)S(1)} %convolution_convert_fusion.16.refs_0_, bf16[512,768]{1,0:T(8,128)(2,1)S(1)} %copy-done.3, bf16[512,768]{1,0:T(8,128)(2,1)S(1)} %copy-done.5, ...), custom_call_target="tpu_custom_call" | custom-call | flops 2013265920 | bytes 12582912 | tf_op jit(solution)/shard_map/pallas_call | solution.py:175
  428.4 25.3 %all-to-all-done.6 = bf16[16,48,768]{2,1,0:T(8,128)(2,1)} async-done(((bf16[16,48,768]{2,1,0:T(8,128)(2,1)}), bf16[16,48,768]{2,1,0:T(8,128)(2,1)}, u32[]{:S(2)}, u32[]{:S(2)}) %all-to-all-start.6) | async-done | bytes 1179680 | tf_op jit(solution)/shard_map/all_to_all | solution.py:303
  453.7 12.3 %fusion.6 = bf16[768,3072]{1,0:T(8,128)(2,1)S(1)} fusion(f32[768,3072]{1,0:T(8,128)} %copy-done.89, bf16[768,768]{1,0:T(8,128)(2,1)} %bitcast.34, bf16[3072,768]{1,0:T(8,128)(2,1)} %collective-permute-done.5, pred[]{:T(512)S(6)} %eq.50, bf16[1,3072,768]{2,1,0:T(8,128)(2,1)} %param.26), kind=kOutput, calls=%fused_computation.10 | convolution fusion | flops 3673423872 | bytes 24772608 | tf_op jit(solution)/shard_map/dot_general | solution.py:62
  466.0 8.6 %fusion.57 = bf16[768,768]{1,0:T(8,128)(2,1)} fusion(bf16[768,3072]{1,0:T(8,128)(2,1)S(1)} %fusion.6, bf16[768,3072]{1,0:T(8,128)(2,1)} %collective-permute-done.4, pred[]{:T(512)S(6)} %eq.50, bf16[1,768,3072]{2,1,0:T(8,128)(2,1)} %param.25), kind=kOutput, calls=%fused_computation.131 | convolution fusion | flops 3626827776 | bytes 15335425 | tf_op jit(solution)/shard_map/dot_general | solution.py:62
  501.0 7.8 %all-to-all-done.7 = bf16[16,48,768]{2,1,0:T(8,128)(2,1)} async-done(((bf16[16,48,768]{2,1,0:T(8,128)(2,1)}), bf16[16,48,768]{2,1,0:T(8,128)(2,1)}, u32[]{:S(2)}, u32[]{:S(2)}) %all-to-all-start.7) | async-done | bytes 1179680 | tf_op jit(solution)/shard_map/all_to_all | solution.py:303
  517.3 18.9 %shard_map.234 = (bf16[512,768]{1,0:T(8,128)(2,1)S(1)}, bf16[512,768]{1,0:T(8,128)(2,1)S(1)}, bf16[512,768]{1,0:T(8,128)(2,1)S(1)}, f32[12,8,1024]{2,1,0:T(8,128)S(1)}) custom-call(bf16[512,768]{1,0:T(8,128)(2,1)S(1)} %convolution_convert_fusion.19.refs_0_, bf16[512,768]{1,0:T(8,128)(2,1)S(1)} %convolution_convert_fusion.18.refs_1_, ...), custom_call_target="tpu_custom_call" | custom-call | flops 2013265920 | bytes 12582912 | tf_op jit(solution)/shard_map/pallas_call | solution.py:175
  550.0 9.8 %broadcast_select_fusion.5 = (bf16[768,1664]{0,1:T(8,128)(2,1)S(1)}, bf16[768,1664]{0,1:T(8,128)(2,1)S(1)}) fusion(pred[]{:T(512)S(6)} %eq.50, bf16[768,768]{0,1:T(8,128)(2,1)S(1)} %copy-done.34, bf16[768,768]{0,1:T(8,128)(2,1)S(1)} %copy-done.48, bf16[1664]{0:T(1024)(128)(2,1)S(1)} %copy-done.68, bf16[768,128]{0,1:T(8,128)(2,1)S(1)} %fusion.126, ...), kind=kLoop, calls=%fused_computation.49 | loop fusion | flops 31948800 | bytes 14945537 | tf_op jit(solution)/shard_map/jit(_where)/select_n | solution.py:451
  568.3 12.4 %add_convert_fusion.1 = (bf16[768,1664]{0,1:T(8,128)(2,1)S(1)}, bf16[768,1664]{0,1:T(8,128)(2,1)}) fusion(bf16[768,1664]{0,1:T(8,128)(2,1)S(1)} %collective-permute-done.9, pred[]{:T(512)S(6)} %eq.50, bf16[768,768]{0,1:T(8,128)(2,1)S(1)} %copy-done.34, bf16[768,768]{0,1:T(8,128)(2,1)S(1)} %copy-done.48, bf16[1664]{0:T(1024)(128)(2,1)S(1)} %copy-done.68, ...), kind=kLoop, calls=%fused_computation.25 | loop fusion | flops 42172416 | bytes 20057344 | tf_op jit(solution)/shard_map/convert_element_type | solution.py:453
  585.2 7.2 all-to-all-start.9
  592.4 8.9 %convolution_convert_fusion.2 = bf16[768,3072]{1,0:T(8,128)(2,1)} fusion(bf16[768,768]{1,0:T(8,128)(2,1)} %bitcast.20, bf16[768,3072]{1,0:T(8,128)(2,1)} %copy-done.91), kind=kOutput, calls=%fused_computation.28 | convolution fusion | flops 3626237952 | bytes 10616832 | tf_op jit(solution)/shard_map/dot_general | solution.py:62
  605.4 8.8 %convolution_convert_fusion.3 = bf16[768,3072]{1,0:T(8,128)(2,1)} fusion(bf16[768,768]{1,0:T(8,128)(2,1)} %bitcast.14, bf16[768,3072]{1,0:T(8,128)(2,1)} %copy-done.92), kind=kOutput, calls=%fused_computation.29 | convolution fusion | flops 3626237952 | bytes 10616832 | tf_op jit(solution)/shard_map/dot_general | solution.py:62
  615.5 8.3 %convolution_convert_fusion = bf16[3072,768]{1,0:T(8,128)(2,1)} fusion(bf16[768,768]{1,0:T(8,128)(2,1)} %bitcast.30, f32[768,3072]{1,0:T(8,128)S(1)} %bitcast.209), kind=kOutput, calls=%fused_computation.26 | convolution fusion | flops 3647471616 | bytes 15335424 | tf_op jit(solution)/shard_map/dot_general | solution.py:62
  623.8 7.4 %collective-permute-start.15 = (bf16[3072,768]{1,0:T(8,128)(2,1)}, bf16[3072,768]{1,0:T(8,128)(2,1)}, u32[]{:S(2)}, u32[]{:S(2)}) collective-permute-start(bf16[3072,768]{1,0:T(8,128)(2,1)} %convolution_convert_fusion), channel_id=1, source_target_pairs={{0,16},{1,17},{2,18},{3,19},{4,20},{5,21},{6,22},{7,23},{8,24},{9,... | collective-permute-start | bytes 14155784 | tf_op jit(solution)/shard_map/ppermute | solution.py:405
  635.2 8.1 %all-to-all-done.9 = bf16[16,48,1664]{2,1,0:T(8,128)(2,1)} async-done(((bf16[16,48,1664]{2,1,0:T(8,128)(2,1)}), bf16[16,48,1664]{2,1,0:T(8,128)(2,1)}, u32[]{:S(2)}, u32[]{:S(2)}) %all-to-all-start.9) | async-done | bytes 2555936 | tf_op jit(solution)/shard_map/all_to_all | solution.py:303
  643.3 12.9 %all-to-all-start.8 = ((bf16[16,48,1664]{2,1,0:T(8,128)(2,1)}), bf16[16,48,1664]{2,1,0:T(8,128)(2,1)S(1)}, u32[]{:S(2)}, u32[]{:S(2)}) async-start(bf16[16,48,1664]{2,1,0:T(8,128)(2,1)} %bitcast.183), calls=%async_computation.8 | async-start | bytes 5111808 | tf_op jit(solution)/shard_map/all_to_all | solution.py:303
  656.3 9.8 %convolution_convert_fusion.1 = bf16[3072,768]{1,0:T(8,128)(2,1)} fusion(bf16[768,768]{1,0:T(8,128)(2,1)} %bitcast.34, f32[768,3072]{1,0:T(8,128)} %copy-done.89), kind=kOutput, calls=%fused_computation.27 | convolution fusion | flops 3647471616 | bytes 15335424 | tf_op jit(solution)/shard_map/dot_general | solution.py:62
  680.8 11.6 %add_bitcast_fusion.1 = f32[1,768,3072]{2,1,0:T(8,128)} fusion(bf16[768,3072]{1,0:T(8,128)(2,1)} %collective-permute-done.12, bf16[768,3072]{1,0:T(8,128)(2,1)} %collective-permute-done.13, bf16[768,3072]{1,0:T(8,128)(2,1)} %convolution_convert_fusion.3, bf16[768,3072]{1,0:T(8,128)(2,1)} %convolution_convert_fusion.2, pred[]{:T(512)S(6)} %eq.50), kind=kLoop, calls=%fused_computation.19 | loop fusion | flops 11796480 | bytes 28311552 | tf_op jit(solution)/shard_map/broadcast_in_dim | solution.py:472
  694.5 11.9 %all-to-all-done.8 = bf16[16,48,1664]{2,1,0:T(8,128)(2,1)S(1)} async-done(((bf16[16,48,1664]{2,1,0:T(8,128)(2,1)}), bf16[16,48,1664]{2,1,0:T(8,128)(2,1)S(1)}, u32[]{:S(2)}, u32[]{:S(2)}) %all-to-all-start.8) | async-done | bytes 2555936 | tf_op jit(solution)/shard_map/all_to_all | solution.py:303
  707.0 9.7 %add_bitcast_fusion = f32[1,3072,768]{2,1,0:T(8,128)} fusion(bf16[3072,768]{1,0:T(8,128)(2,1)} %collective-permute-done.14, bf16[3072,768]{1,0:T(8,128)(2,1)} %collective-permute-done.15, bf16[3072,768]{1,0:T(8,128)(2,1)} %convolution_convert_fusion.1, bf16[3072,768]{1,0:T(8,128)(2,1)} %convolution_convert_fusion, pred[]{:T(512)S(6)} %eq.50), kind=kLoop, calls=%fused_computation.18 | loop fusion | flops 11796480 | bytes 28311552 | tf_op jit(solution)/shard_map/broadcast_in_dim | solution.py:472
  (366 shorter events, 236.8 us)
Async XLA Ops:
  7.2 72.9 %all-gather.3.cloned.1.call-start = ((), (), s32[]{:S(2)}) async-start(), calls=%async_computation.10 | async-start | bytes 2715648 | tf_op jit(solution)/shard_map/all_gather | solution.py:276
  11.6 1.5 collective-permute-start
  14.0 160.4 %all-gather.5.cloned.1.call-start = ((), (), s32[]{:S(2)}) async-start(), calls=%async_computation.11 | async-start | bytes 2715648 | tf_op jit(solution)/shard_map/all_gather | solution.py:276
  84.7 12.8 %collective-permute-start.1 = (bf16[768,1664]{0,1:T(8,128)(2,1)S(1)}, bf16[768,1664]{0,1:T(8,128)(2,1)}, u32[]{:S(2)}, u32[]{:S(2)}) collective-permute-start(bf16[768,1664]{0,1:T(8,128)(2,1)S(1)} %copy.95), channel_id=1, source_target_pairs={{0,16},{16,0},{1,17},{17,1},{2,18},{18,2},{3,19},{19,3},{4,20},{20... | collective-permute-start | bytes 7667720 | tf_op jit(solution)/shard_map/ppermute | solution.py:228
  84.8 4.4 collective-permute-start.2
  85.3 11.6 %collective-permute-start.3 = (s32[512]{0:T(512)S(1)}, s32[512]{0:T(512)S(1)}, u32[]{:S(2)}, u32[]{:S(2)}) collective-permute-start(s32[512]{0:T(512)S(1)} %bitcast.201), channel_id=1, source_target_pairs={{0,16},{16,0},{1,17},{17,1},{2,18},{18,2},{3,19},{19,3},{4,20},{20... | collective-permute-start | bytes 6152 | tf_op jit(solution)/shard_map/ppermute | solution.py:228
  85.4 99.5 %collective-permute-start.5 = (bf16[3072,768]{1,0:T(8,128)(2,1)}, bf16[3072,768]{1,0:T(8,128)(2,1)}, u32[]{:S(2)}, u32[]{:S(2)}) collective-permute-start(bf16[3072,768]{1,0:T(8,128)(2,1)} %bitcast.206), channel_id=1, source_target_pairs={{0,16},{16,0},{1,17},{17,1},{2,18},{18,2},{3,19},{19,3},{4,20},{20... | collective-permute-start | bytes 14155784 | tf_op jit(solution)/shard_map/ppermute | solution.py:228
  85.8 93.0 %collective-permute-start.4 = (bf16[768,3072]{1,0:T(8,128)(2,1)}, bf16[768,3072]{1,0:T(8,128)(2,1)}, u32[]{:S(2)}, u32[]{:S(2)}) collective-permute-start(bf16[768,3072]{1,0:T(8,128)(2,1)} %bitcast.207), channel_id=1, source_target_pairs={{0,16},{16,0},{1,17},{17,1},{2,18},{18,2},{3,19},{19,3},{4,20},{20... | collective-permute-start | bytes 14155784 | tf_op jit(solution)/shard_map/ppermute | solution.py:228
  96.9 267.6 %copy-start.63 = (s32[512]{0:T(512)}, s32[512]{0:T(512)S(1)}, u32[]{:S(2)}) copy-start(s32[512]{0:T(512)S(1)} %get-tuple-element.118) | copy-start | bytes 6148
  97.4 321.0 %copy-start.75 = (s32[512]{0:T(512)}, s32[512]{0:T(512)S(1)}, u32[]{:S(2)}) copy-start(s32[512]{0:T(512)S(1)} %get-tuple-element.139) | copy-start | bytes 6148
  116.4 62.4 %all-to-all-start = ((bf16[16,48,768]{2,1,0:T(8,128)(2,1)}), bf16[16,48,768]{2,1,0:T(8,128)(2,1)}, u32[]{:S(2)}, u32[]{:S(2)}) async-start(bf16[16,48,768]{2,1,0:T(8,128)(2,1)} %bitcast.187), calls=%async_computation | async-start | bytes 2359296 | tf_op jit(solution)/shard_map/all_to_all | solution.py:303
  178.8 30.9 %collective-permute-start.6 = (bf16[768,1664]{0,1:T(8,128)(2,1)}, bf16[768,1664]{0,1:T(8,128)(2,1)}, u32[]{:S(2)}, u32[]{:S(2)}) collective-permute-start(bf16[768,1664]{0,1:T(8,128)(2,1)} %copy.99), channel_id=1, source_target_pairs={{0,16},{16,0},{1,17},{17,1},{2,18},{18,2},{3,19},{19,3},{4,20},{20... | collective-permute-start | bytes 7667720 | tf_op jit(solution)/shard_map/ppermute | solution.py:228
  197.3 30.6 %all-to-all-start.1 = ((bf16[16,48,768]{2,1,0:T(8,128)(2,1)}), bf16[16,48,768]{2,1,0:T(8,128)(2,1)}, u32[]{:S(2)}, u32[]{:S(2)}) async-start(bf16[16,48,768]{2,1,0:T(8,128)(2,1)} %bitcast.186), calls=%async_computation.1 | async-start | bytes 2359296 | tf_op jit(solution)/shard_map/all_to_all | solution.py:303
  213.2 203.7 %copy-start.66 = (f32[768]{0:T(1024)}, f32[768]{0:T(1024)S(1)}, u32[]{:S(2)}) copy-start(f32[768]{0:T(1024)S(1)} %get-tuple-element.83) | copy-start | bytes 9220
  214.8 203.6 %copy-start.71 = (f32[512]{0:T(512)}, f32[512]{0:T(512)S(1)}, u32[]{:S(2)}) copy-start(f32[512]{0:T(512)S(1)} %select_reduce_fusion.1) | copy-start | bytes 6148
  250.6 35.9 %all-to-all-start.2 = ((bf16[16,48,768]{2,1,0:T(8,128)(2,1)}), bf16[16,48,768]{2,1,0:T(8,128)(2,1)}, u32[]{:S(2)}, u32[]{:S(2)}) async-start(bf16[16,48,768]{2,1,0:T(8,128)(2,1)} %bitcast.190), calls=%async_computation.2 | async-start | bytes 2359296 | tf_op jit(solution)/shard_map/all_to_all | solution.py:303
  286.5 34.8 %all-to-all-start.4 = ((bf16[16,48,768]{2,1,0:T(8,128)(2,1)}), bf16[16,48,768]{2,1,0:T(8,128)(2,1)}, u32[]{:S(2)}, u32[]{:S(2)}) async-start(bf16[16,48,768]{2,1,0:T(8,128)(2,1)} %bitcast.191), calls=%async_computation.4 | async-start | bytes 2359296 | tf_op jit(solution)/shard_map/all_to_all | solution.py:303
  321.3 32.2 %all-to-all-start.3 = ((bf16[16,48,768]{2,1,0:T(8,128)(2,1)}), bf16[16,48,768]{2,1,0:T(8,128)(2,1)}, u32[]{:S(2)}, u32[]{:S(2)}) async-start(bf16[16,48,768]{2,1,0:T(8,128)(2,1)} %bitcast.192), calls=%async_computation.3 | async-start | bytes 2359296 | tf_op jit(solution)/shard_map/all_to_all | solution.py:303
  353.5 33.2 %all-to-all-start.5 = ((bf16[16,48,768]{2,1,0:T(8,128)(2,1)}), bf16[16,48,768]{2,1,0:T(8,128)(2,1)}, u32[]{:S(2)}, u32[]{:S(2)}) async-start(bf16[16,48,768]{2,1,0:T(8,128)(2,1)} %bitcast.188), calls=%async_computation.5 | async-start | bytes 2359296 | tf_op jit(solution)/shard_map/all_to_all | solution.py:303
  421.3 32.4 %all-to-all-start.6 = ((bf16[16,48,768]{2,1,0:T(8,128)(2,1)}), bf16[16,48,768]{2,1,0:T(8,128)(2,1)}, u32[]{:S(2)}, u32[]{:S(2)}) async-start(bf16[16,48,768]{2,1,0:T(8,128)(2,1)} %bitcast.189), calls=%async_computation.6 | async-start | bytes 2359296 | tf_op jit(solution)/shard_map/all_to_all | solution.py:303
  474.6 34.1 %all-to-all-start.7 = ((bf16[16,48,768]{2,1,0:T(8,128)(2,1)}), bf16[16,48,768]{2,1,0:T(8,128)(2,1)}, u32[]{:S(2)}, u32[]{:S(2)}) async-start(bf16[16,48,768]{2,1,0:T(8,128)(2,1)} %bitcast.185), calls=%async_computation.7 | async-start | bytes 2359296 | tf_op jit(solution)/shard_map/all_to_all | solution.py:303
  559.8 4.9 collective-permute-start.9
  559.9 8.5 %collective-permute-start.10 = (bf16[768,1664]{0,1:T(8,128)(2,1)S(1)}, bf16[768,1664]{0,1:T(8,128)(2,1)S(1)}, u32[]{:S(2)}, u32[]{:S(2)}) collective-permute-start(bf16[768,1664]{0,1:T(8,128)(2,1)S(1)} %get-tuple-element.117), channel_id=1, source_target_pairs={{0,16},{16,0},{1,17},{17,1},{2,18},{18,2},{3,19},{19,3},{4,20},{20... | collective-permute-start | bytes 7667720 | tf_op jit(solution)/shard_map/ppermute | solution.py:228
  585.2 58.1 %all-to-all-start.9 = ((bf16[16,48,1664]{2,1,0:T(8,128)(2,1)}), bf16[16,48,1664]{2,1,0:T(8,128)(2,1)}, u32[]{:S(2)}, u32[]{:S(2)}) async-start(bf16[16,48,1664]{2,1,0:T(8,128)(2,1)} %bitcast.184), calls=%async_computation.9 | async-start | bytes 5111808 | tf_op jit(solution)/shard_map/all_to_all | solution.py:303
  601.3 79.5 %collective-permute-start.13 = (bf16[768,3072]{1,0:T(8,128)(2,1)}, bf16[768,3072]{1,0:T(8,128)(2,1)}, u32[]{:S(2)}, u32[]{:S(2)}) collective-permute-start(bf16[768,3072]{1,0:T(8,128)(2,1)} %convolution_convert_fusion.2), channel_id=1, source_target_pairs={{0,16},{1,17},{2,18},{3,19},{4,20},{5,21},{6,22},{7,23},{8,24},{9,... | collective-permute-start | bytes 14155784 | tf_op jit(solution)/shard_map/ppermute | solution.py:404
  614.2 66.6 %collective-permute-start.12 = (bf16[768,3072]{1,0:T(8,128)(2,1)}, bf16[768,3072]{1,0:T(8,128)(2,1)}, u32[]{:S(2)}, u32[]{:S(2)}) collective-permute-start(bf16[768,3072]{1,0:T(8,128)(2,1)} %convolution_convert_fusion.3), channel_id=1, source_target_pairs={{16,0},{17,1},{18,2},{19,3},{20,4},{21,5},{22,6},{23,7},{24,8},{25... | collective-permute-start | bytes 14155784 | tf_op jit(solution)/shard_map/ppermute | solution.py:404
  623.8 83.1 %collective-permute-start.15 = (bf16[3072,768]{1,0:T(8,128)(2,1)}, bf16[3072,768]{1,0:T(8,128)(2,1)}, u32[]{:S(2)}, u32[]{:S(2)}) collective-permute-start(bf16[3072,768]{1,0:T(8,128)(2,1)} %convolution_convert_fusion), channel_id=1, source_target_pairs={{0,16},{1,17},{2,18},{3,19},{4,20},{5,21},{6,22},{7,23},{8,24},{9,... | collective-permute-start | bytes 14155784 | tf_op jit(solution)/shard_map/ppermute | solution.py:405
  643.3 63.1 %all-to-all-start.8 = ((bf16[16,48,1664]{2,1,0:T(8,128)(2,1)}), bf16[16,48,1664]{2,1,0:T(8,128)(2,1)S(1)}, u32[]{:S(2)}, u32[]{:S(2)}) async-start(bf16[16,48,1664]{2,1,0:T(8,128)(2,1)} %bitcast.183), calls=%async_computation.8 | async-start | bytes 5111808 | tf_op jit(solution)/shard_map/all_to_all | solution.py:303
  666.1 40.8 %collective-permute-start.14 = (bf16[3072,768]{1,0:T(8,128)(2,1)}, bf16[3072,768]{1,0:T(8,128)(2,1)}, u32[]{:S(2)}, u32[]{:S(2)}) collective-permute-start(bf16[3072,768]{1,0:T(8,128)(2,1)} %convolution_convert_fusion.1), channel_id=1, source_target_pairs={{16,0},{17,1},{18,2},{19,3},{20,4},{21,5},{22,6},{23,7},{24,8},{25... | collective-permute-start | bytes 14155784 | tf_op jit(solution)/shard_map/ppermute | solution.py:405
  667.4 9.6 %collective-permute-start.7 = (bf16[512,768]{1,0:T(8,128)(2,1)S(1)}, bf16[512,768]{1,0:T(8,128)(2,1)S(1)}, u32[]{:S(2)}, u32[]{:S(2)}) collective-permute-start(bf16[512,768]{1,0:T(8,128)(2,1)S(1)} %copy-done.61), channel_id=1, source_target_pairs={{0,16},{16,0},{1,17},{17,1},{2,18},{18,2},{3,19},{19,3},{4,20},{20... | collective-permute-start | bytes 2359304 | tf_op jit(solution)/shard_map/ppermute | solution.py:228
  677.0 2.3 collective-permute-start.8
  706.9 9.8 %collective-permute-start.11 = (f32[48,1664]{1,0:T(8,128)S(1)}, f32[48,1664]{1,0:T(8,128)S(1)}, u32[]{:S(2)}, u32[]{:S(2)}) collective-permute-start(f32[48,1664]{1,0:T(8,128)S(1)} %broadcast_select_fusion.32), channel_id=1, source_target_pairs={{0,16},{16,0},{1,17},{17,1},{2,18},{18,2},{3,19},{19,3},{4,20},{20... | collective-permute-start | bytes 958472 | tf_op jit(solution)/shard_map/ppermute | solution.py:228
  (92 other events, 1399.7 us)
Sparse Core Ops, SparseCore 0:
  14.0 66.0 all-gather.2
  97.6 76.7 all-gather.4
